TPU v7x, 256 devices: a whole 4x4x8 slice. The times are simulated.
256 devices in a mesh: tm: 32 (over y, z_lo, core), head: 8 (over z_hi, x).
Axes of the slice: x: 4, y: 4, z: 8 (z_hi: 2, z_lo: 4; z = z_hi * 4 + z_lo), core: 2. Of those that a mesh axis runs over, the one named last changes fastest.
Arguments:
- latents: bfloat16 [16384, 3072], P(('tm', 'head')), may hold values from -6 to 6
- cotangent: bfloat16 [16384, 3072], P(('tm', 'head')), may hold values from -6 to 6
- norm_gain: float32 [3072], replicated, may hold values from 0.1 to 1.9
- w_qkv: bfloat16 [3072, 3, 3072], P(None, None, 'head'), may hold values from -0.114763592 to 0.114763592
- w_out: bfloat16 [3072, 3072], P('head'), may hold values from -0.109375 to 0.109375
Outputs:
- input_grad: bfloat16 [16384, 3072], P(('tm', 'head'))
All inputs are finite; a program needn't handle non-finite values.
Results may differ from a plain program's by a relative error of at most 0.012.
Values may be sent and summed in bfloat16 or wider, within the bound.
A program may use at most 128 MiB of HBM per device.

v0:
```python
import jax
import jax.numpy as jnp
from jax import lax
from jax.sharding import PartitionSpec as P

HEAD_DIM = 128


EPSILON = 1e-06


def from_behind(block, axis, distance):
    devices = range(lax.axis_size(axis))
    route = [(i - distance, i) for i in devices if i - distance in devices]
    return lax.ppermute(block, axis, route)


def scores_of(queries, keys):
    return jnp.einsum(
        "phe,khe->hpk", queries, keys, preferred_element_type=jnp.float32
    ) * HEAD_DIM ** (-0.5)


def shards(latents, cotangent, norm_gain, w_qkv, w_out):
    feature_count = latents.shape[1]
    local_width = w_qkv.shape[2]
    heads_here = local_width // HEAD_DIM
    scale = HEAD_DIM ** (-0.5)
    latent_f = latents.astype(jnp.float32)
    inv_rms = lax.rsqrt(jnp.mean(latent_f * latent_f, axis=-1, keepdims=True) + EPSILON)
    normed = latent_f * inv_rms
    hidden = (normed * norm_gain).astype(jnp.bfloat16)
    flat_w = w_qkv.reshape(feature_count, 3 * local_width)
    projected = jnp.dot(
        lax.all_gather(hidden, "head", axis=0, tiled=True),
        flat_w,
        preferred_element_type=jnp.float32,
    ).astype(jnp.bfloat16)
    frame_len = projected.shape[0]
    shape3 = (frame_len, heads_here, HEAD_DIM)
    queries = projected[:, :local_width].reshape(shape3)
    keys_own = projected[:, local_width : 2 * local_width].reshape(shape3)
    values_own = projected[:, 2 * local_width :].reshape(shape3)
    keys_prev, values_prev = from_behind((keys_own, values_own), "tm", 1)
    has_prev = (lax.axis_index("tm") > 0).astype(jnp.float32)
    grad_attn = (
        lax.dot_general(
            lax.all_gather(cotangent, "head", axis=0, tiled=True),
            w_out,
            (((1,), (1,)), ((), ())),
            preferred_element_type=jnp.float32,
        )
        .astype(jnp.bfloat16)
        .reshape(shape3)
    )
    own_s = scores_of(queries, keys_own)
    prev_s = scores_of(queries, keys_prev)
    row_top = jnp.maximum(
        jnp.max(own_s, axis=-1), jnp.where(has_prev > 0.5, jnp.max(prev_s, axis=-1), -1e30)
    )
    own_e = jnp.exp(own_s - row_top[..., None])
    prev_e = jnp.exp(prev_s - row_top[..., None]) * has_prev
    row_total = jnp.sum(own_e, axis=-1) + jnp.sum(prev_e, axis=-1)
    own_p = own_e / row_total[..., None]
    prev_p = prev_e / row_total[..., None]
    own_dp = jnp.einsum("phe,khe->hpk", grad_attn, values_own, preferred_element_type=jnp.float32)
    prev_dp = jnp.einsum("phe,khe->hpk", grad_attn, values_prev, preferred_element_type=jnp.float32)
    row_delta = jnp.sum(own_p * own_dp, axis=-1) + jnp.sum(prev_p * prev_dp, axis=-1)
    own_ds = (own_p * (own_dp - row_delta[..., None]) * scale).astype(jnp.bfloat16)
    prev_ds = (prev_p * (prev_dp - row_delta[..., None]) * scale).astype(jnp.bfloat16)
    grad_query = (
        jnp.einsum("hpk,khe->phe", own_ds, keys_own, preferred_element_type=jnp.float32)
        + jnp.einsum("hpk,khe->phe", prev_ds, keys_prev, preferred_element_type=jnp.float32)
    ).astype(jnp.bfloat16)
    key_own_g = jnp.einsum("hpk,phe->khe", own_ds, queries, preferred_element_type=jnp.float32)
    value_own_g = jnp.einsum(
        "hpk,phe->khe", own_p.astype(jnp.bfloat16), grad_attn, preferred_element_type=jnp.float32
    )
    key_back_g = jnp.einsum(
        "hpk,phe->khe", prev_ds, queries, preferred_element_type=jnp.float32
    ).astype(jnp.bfloat16)
    value_back_g = jnp.einsum(
        "hpk,phe->khe", prev_p.astype(jnp.bfloat16), grad_attn, preferred_element_type=jnp.float32
    ).astype(jnp.bfloat16)
    key_next, value_next = from_behind((key_back_g, value_back_g), "tm", -1)
    grad_key = (key_own_g + key_next.astype(jnp.float32)).astype(jnp.bfloat16)
    grad_value = (value_own_g + value_next.astype(jnp.float32)).astype(jnp.bfloat16)
    grad_qkv = jnp.concatenate(
        [
            grad_query.reshape(frame_len, local_width),
            grad_key.reshape(frame_len, local_width),
            grad_value.reshape(frame_len, local_width),
        ],
        axis=1,
    )
    grad_hidden = lax.psum_scatter(
        lax.dot_general(
            grad_qkv, flat_w, (((1,), (1,)), ((), ())), preferred_element_type=jnp.float32
        ).astype(jnp.bfloat16),
        "head",
        scatter_dimension=0,
        tiled=True,
    ).astype(jnp.float32)
    grad_normed = grad_hidden * norm_gain
    inner = jnp.mean(grad_normed * normed, axis=-1, keepdims=True)
    result = cotangent.astype(jnp.float32) + inv_rms * (grad_normed - normed * inner)
    return result.astype(jnp.bfloat16)


def solution(mesh):
    return jax.shard_map(
        shards,
        mesh=mesh,
        in_specs=(
            P(("tm", "head"), None),
            P(("tm", "head"), None),
            P(),
            P(None, None, "head"),
            P("head", None),
        ),
        out_specs=P(("tm", "head"), None),
        check_vma=False,
    )
```

profile of v0, /device:TPU:1, one launch (start us, length us, event | category | flops | bytes accessed | tf_op | source)
XLA Modules:
  0.0 347.3 jit_solution(16157256869247840403)
XLA Ops:
  6.5 0.0 copy-start
  6.5 1.3 fusion.33
  7.9 1.9 fusion.27
  9.8 0.0 all-gather.3.cloned.1.call-update
  9.8 0.0 all-gather.5.cloned.1.call-start
  9.9 0.7 all-gather.5.cloned.1.call-update
  10.6 0.0 reduce-scatter.2.cloned.1.call-start
  10.6 10.3 %copy.24 = bf16[3072,3,384]{0,2,1:T(8,128)(2,1)} copy(bf16[3072,3,384]{2,0,1:T(8,128)(2,1)} %param.8) | data formatting | bytes 14155776 | tf_op args[3]
  20.9 84.3 %all-gather.3.cloned.1.call-done = bf16[512,3072]{1,0:T(8,128)(2,1)} async-done(((bf16[64,3072]{1,0:T(8,128)(2,1)}), bf16[512,3072]{1,0:T(8,128)(2,1)}) %all-gather.3.cloned.1.call-update) | async-done | bytes 3145744 | tf_op jit(solution)/shard_map/all_gather | solution.py:35
  105.2 8.2 %convolution_convert_fusion.1 = bf16[512,1152]{1,0:T(8,128)(2,1)S(1)} fusion(bf16[512,3072]{1,0:T(8,128)(2,1)} %all-gather.3.cloned.1.call-done, bf16[3072,1152]{0,1:T(8,128)(2,1)} %bitcast.47), kind=kOutput, calls=%fused_computation.7 | convolution fusion | flops 3624468480 | bytes 11403264 | tf_op jit(solution)/shard_map/dot_general | solution.py:34
  113.4 0.9 fusion.39
  114.3 0.2 copy.31
  114.5 0.9 copy.34
  115.4 1.2 copy.25
  116.6 0.9 copy.29
  117.5 3.2 collective-permute-start
  120.8 1.9 collective-permute-start.1
  122.7 73.3 %all-gather.5.cloned.1.call-done = bf16[512,3072]{1,0:T(8,128)(2,1)} async-done(((bf16[64,3072]{1,0:T(8,128)(2,1)}), bf16[512,3072]{1,0:T(8,128)(2,1)}) %all-gather.5.cloned.1.call-update) | async-done | bytes 3145744 | tf_op jit(solution)/shard_map/all_gather | solution.py:48
  196.0 3.3 convolution_convert_fusion.3
  199.3 0.0 copy-start.4
  199.3 2.3 fusion.40
  201.7 0.2 copy.26
  201.9 0.6 multiply_reduce_fusion.3
  202.5 0.0 collective-permute-done
  202.5 1.6 multiply_reduce_fusion.2
  204.1 0.0 copy-start.5
  204.1 1.1 fusion.3
  205.3 0.9 fusion.16
  206.2 3.2 collective-permute-start.3
  209.4 0.0 collective-permute-done.1
  209.4 2.7 multiply_reduce_fusion
  212.2 2.0 multiply_convert_fusion
  214.2 0.4 fusion.41
  214.6 0.6 fusion.15
  215.2 1.9 collective-permute-start.2
  217.1 0.0 slice-start
  217.1 1.6 fusion.14
  218.7 0.0 slice-start.1
  218.7 0.0 collective-permute-done.3
  218.7 0.9 add_convert_fusion
  219.6 4.7 %collective-permute-done.2 = bf16[512,3,128]{0,2,1:T(8,128)(2,1)S(1)} collective-permute-done((bf16[512,3,128]{0,2,1:T(8,128)(2,1)S(1)}, bf16[512,3,128]{0,2,1:T(8,128)(2,1)S(1)}, u32[]{:S(2)}, u32[]{:S(2)}) %collective-permute-start.2) | collective-permute-done | bytes 393248 | tf_op jit(solution)/shard_map/ppermute | solution.py:15
  224.3 0.6 add_convert_fusion.1
  225.0 5.8 %convolution_convert_fusion = bf16[512,3072]{1,0:T(8,128)(2,1)} fusion(bf16[3072,1152]{0,1:T(8,128)(2,1)S(1)} %bitcast.50, bf16[512,384]{0,1:T(8,128)(2,1)S(1)} %bitcast.62, bf16[512,384]{0,1:T(8,128)(2,1)S(1)} %bitcast.57, bf16[512,384]{0,1:T(8,128)(2,1)S(1)} %bitcast.56), kind=kOutput, calls=%fused_computation | convolution fusion | flops 3628990464 | bytes 11403264 | tf_op jit(solution)/shard_map/dot_general | solution.py:97
  230.8 0.0 reduce-scatter.2.cloned.1.call-update
  230.8 106.6 %reduce-scatter.2.cloned.1.call-done = bf16[64,3072]{1,0:T(8,128)(2,1)} async-done(((bf16[512,3072]{1,0:T(8,128)(2,1)}), bf16[64,3072]{1,0:T(8,128)(2,1)}) %reduce-scatter.2.cloned.1.call-update) | async-done | bytes 393232 | tf_op jit(solution)/shard_map/reduce_scatter | solution.py:96
  337.4 0.0 copy-done.2
  337.4 1.3 fusion.28
  338.7 2.0 fusion.32
  (19 shorter events, 0.1 us)
Async XLA Ops:
  6.5 189.5 %copy-start = (bf16[384,3072]{1,0:T(8,128)(2,1)S(1)}, bf16[384,3072]{1,0:T(8,128)(2,1)}, u32[]{:S(2)}) copy-start(bf16[384,3072]{1,0:T(8,128)(2,1)} %param.9) | copy-start | bytes 7077892
  6.5 98.6 %all-gather.3.cloned.1.call-start = ((), (), s32[]{:S(2)}) async-start(), calls=%async_computation.1 | async-start | bytes 3538944 | tf_op jit(solution)/shard_map/all_gather | solution.py:35
  9.8 186.2 %all-gather.5.cloned.1.call-start = ((), (), s32[]{:S(2)}) async-start(), calls=%async_computation.2 | async-start | bytes 3538944 | tf_op jit(solution)/shard_map/all_gather | solution.py:48
  10.6 326.9 %reduce-scatter.2.cloned.1.call-start = ((), (), s32[]{:S(2)}) async-start(), calls=%async_computation.3 | async-start | bytes 3538944 | tf_op jit(solution)/shard_map/reduce_scatter | solution.py:96
  117.5 85.0 %collective-permute-start = (bf16[512,3,128]{2,0,1:T(8,128)(2,1)}, bf16[512,3,128]{2,0,1:T(8,128)(2,1)}, u32[]{:S(2)}, u32[]{:S(2)}) collective-permute-start(bf16[512,3,128]{2,0,1:T(8,128)(2,1)} %copy.29), channel_id=1, source_target_pairs={{0,8},{8,16},{16,24},{24,32},{32,40},{40,48},{48,56},{56,64},{64,7... | collective-permute-start | bytes 1179656 | tf_op jit(solution)/shard_map/ppermute | solution.py:15
  120.8 88.7 %collective-permute-start.1 = (bf16[512,3,128]{2,0,1:T(8,128)(2,1)}, bf16[512,3,128]{2,0,1:T(8,128)(2,1)}, u32[]{:S(2)}, u32[]{:S(2)}) collective-permute-start(bf16[512,3,128]{2,0,1:T(8,128)(2,1)} %copy.34), channel_id=1, source_target_pairs={{0,8},{8,16},{16,24},{24,32},{32,40},{40,48},{48,56},{56,64},{64,7... | collective-permute-start | bytes 1179656 | tf_op jit(solution)/shard_map/ppermute | solution.py:15
  199.3 2.4 copy-start.4
  204.1 1.2 copy-start.5
  205.3 4.1 %copy-start.1 = (f32[3,512,512]{1,2,0:T(8,128)S(1)}, f32[3,512,512]{1,2,0:T(8,128)}, u32[]{:S(2)}) copy-start(f32[3,512,512]{1,2,0:T(8,128)} %fusion.40) | copy-start | bytes 9437188
  206.2 12.5 %collective-permute-start.3 = (bf16[512,3,128]{0,2,1:T(8,128)(2,1)S(1)}, bf16[512,3,128]{0,2,1:T(8,128)(2,1)S(1)}, u32[]{:S(2)}, u32[]{:S(2)}) collective-permute-start(bf16[512,3,128]{0,2,1:T(8,128)(2,1)S(1)} %fusion.16), channel_id=1, source_target_pairs={{8,0},{16,8},{24,16},{32,24},{40,32},{48,40},{56,48},{64,56},{72,6... | collective-permute-start | bytes 1179656 | tf_op jit(solution)/shard_map/ppermute | solution.py:15
  215.2 9.1 %collective-permute-start.2 = (bf16[512,3,128]{0,2,1:T(8,128)(2,1)S(1)}, bf16[512,3,128]{0,2,1:T(8,128)(2,1)S(1)}, u32[]{:S(2)}, u32[]{:S(2)}) collective-permute-start(bf16[512,3,128]{0,2,1:T(8,128)(2,1)S(1)} %fusion.15), channel_id=1, source_target_pairs={{8,0},{16,8},{24,16},{32,24},{40,32},{48,40},{56,48},{64,56},{72,6... | collective-permute-start | bytes 1179656 | tf_op jit(solution)/shard_map/ppermute | solution.py:15
  217.1 7.8 %slice-start = ((s8[7077888]{0:T(1024)(128)(4,1)}), s8[2883584]{0:T(1024)(128)(4,1)S(1)}, s32[]{:S(2)}) async-start(s8[7077888]{0:T(1024)(128)(4,1)} %bitcast.48), calls=%async_computation.4 | async-start | bytes 5767168
  218.7 6.2 %slice-start.1 = ((s8[7077888]{0:T(1024)(128)(4,1)}), s8[4194304]{0:T(1024)(128)(4,1)S(1)}, s32[]{:S(2)}) async-start(s8[7077888]{0:T(1024)(128)(4,1)} %bitcast.48), calls=%async_computation.5 | async-start | bytes 8388608
  230.8 106.7 %copy-start.2 = (bf16[64,3072]{1,0:T(8,128)(2,1)S(1)}, bf16[64,3072]{1,0:T(8,128)(2,1)}, u32[]{:S(2)}) copy-start(bf16[64,3072]{1,0:T(8,128)(2,1)} %param.5) | copy-start | bytes 1179652
  230.8 106.7 %copy-start.6 = (f32[3072]{0:T(1024)S(1)}, f32[3072]{0:T(1024)}, u32[]{:S(2)}) copy-start(f32[3072]{0:T(1024)} %param.7) | copy-start | bytes 36868
  230.8 107.9 %copy-start.3 = (bf16[64,3072]{1,0:T(8,128)(2,1)S(1)}, bf16[64,3072]{1,0:T(8,128)(2,1)}, u32[]{:S(2)}) copy-start(bf16[64,3072]{1,0:T(8,128)(2,1)} %param.6) | copy-start | bytes 1179652
Sparse Core Ops, SparseCore 0:
  10.0 95.1 all-gather.2
  107.8 88.1 all-gather.4
  230.9 106.4 reduce-scatter.1
where the time goes:
time: 348 us; the launch traced here: 347 us
  waiting for transfers between devices  270 us (78%)
  matrix products  29.6 us (9%)
  local copies, waits for them, and re-layouts  14.6 us (4%)
  between operations  13.4 us (4%)
  starting transfers between devices  10.3 us (3%)
  other arithmetic  9.7 us (3%)
    reduce_scatter x1, waiting for transfers between devices, shards(): lax.psum_scatter(lax.dot_general(grad_qkv, flat_w, (((1,), (1,)), ((), ()...  107 us
    all_gather x1, waiting for transfers between devices, shards(): lax.all_gather(hidden, 'head', axis=0, tiled=True)  84.3 us
    all_gather x1, waiting for transfers between devices, shards(): lax.all_gather(cotangent, 'head', axis=0, tiled=True)  73.3 us
    unnamed x19, local copies, waits for them, and re-layouts  10.3 us
    ppermute x4, starting transfers between devices, from_behind(): return lax.ppermute(block, axis, route)  10.3 us
    dot_general x1, matrix products, shards(): jnp.dot(lax.all_gather(hidden, 'head', axis=0, tiled=True), flat_w, prefe...  8.22 us
  transfers between devices with their start and end apart: 7, of which 4 were waited for; matrix products, arithmetic and copies ran while one was open for 12% of the time, Pallas kernels for 0%

commit v1 on v0

v1 whole, which is shorter than its diff:
```python
import functools

import jax
import jax.numpy as jnp
from jax import lax
from jax.experimental import pallas as pl
from jax.experimental.pallas import tpu as pltpu
from jax.sharding import PartitionSpec as P

EPSILON = 1e-06
MESH = pl.DeviceIdType.MESH
D = 3072
HEAD_DIM = 128
HEADS_HERE = 3
WIDTH = HEADS_HERE * HEAD_DIM
BLOCK = 64
HALF = BLOCK // 2
FRAME = 512
PAIR = 2 * BLOCK
COLS = D // 2
N_TM = 32
X = 4
SCALE = HEAD_DIM ** (-0.5)
BF = jnp.bfloat16
F32 = jnp.float32


def nt(a, b):
    return lax.dot_general(a, b, (((1,), (1,)), ((), ())), preferred_element_type=F32)


def nn(a, b):
    return jnp.dot(a, b, preferred_element_type=F32)


def kernel(
    lat_h, cot_h, gain_h, wqkv_h, wout_h, out_ref,
    lat, gain, wq, wo, hid, cot, inv, q, kv, kt, probs, acc_k, acc_v, back_s, back_r, g,
    part, ra, rb, rl, rr, zs, rz, ga_s, grad,
    ld_sem, gs_sem, gr_sem, kvs_sem, kvr_sem, bs_sem, br_sem, rs_sem, rr_sem, zs_sem, zr_sem,
):
    tm = lax.axis_index("tm")
    head = lax.axis_index("head")
    x = lax.rem(head, X)
    base = head - x
    right = (tm, base + lax.rem(x + 1, X))
    left = (tm, base + lax.rem(x + X - 1, X))
    across = (tm, lax.rem(head + X, 2 * X))
    after = (lax.rem(tm + 1, N_TM), head)
    before = (lax.rem(tm + N_TM - 1, N_TM), head)

    barrier = pltpu.get_barrier_semaphore()
    for peer in (right, left, across, after, before):
        pl.semaphore_signal(barrier, inc=1, device_id=peer, device_id_type=MESH)

    loads = [
        pltpu.make_async_copy(lat_h, lat, ld_sem.at[0]),
        pltpu.make_async_copy(gain_h, gain, ld_sem.at[1]),
        pltpu.make_async_copy(cot_h, cot.at[pl.ds(0, BLOCK)], ld_sem.at[2]),
        pltpu.make_async_copy(wqkv_h, wq, ld_sem.at[3]),
        pltpu.make_async_copy(wout_h, wo, ld_sem.at[4]),
    ]
    for load in loads:
        load.start()
    loads[0].wait()
    loads[1].wait()
    for r in range(4):
        rows = pl.ds(r * 16, 16)
        lf = lat[rows].astype(F32)
        scale = lax.rsqrt(jnp.mean(lf * lf, axis=-1, keepdims=True) + EPSILON)
        inv[rows] = jnp.broadcast_to(scale, (16, 128))
        hid[rows] = (lf * scale * gain[...]).astype(BF)
    pl.semaphore_wait(barrier, 5)

    sent = []

    def push(src, dst, s_sem, r_sem, peer):
        copy = pltpu.make_async_remote_copy(
            src_ref=src, dst_ref=dst, send_sem=s_sem, recv_sem=r_sem, device_id=peer, device_id_type=MESH
        )
        copy.start()
        sent.append(copy)
        return copy

    def chunk(slot, c):
        return pl.ds(slot * BLOCK + c * HALF, HALF)

    bufs = (hid, cot)
    moves = {}

    def gather_push(a, src_slot, dst_slot, c, peer):
        i = dst_slot * 2 + c
        moves[a, dst_slot, c] = push(
            bufs[a].at[chunk(src_slot, c)], bufs[a].at[chunk(dst_slot, c)], gs_sem.at[a, i], gr_sem.at[a, i], peer
        )

    def got(a, slot, c):
        moves[a, slot, c].wait_recv()

    def spread(a, zz, cs):
        for c in cs:
            gather_push(a, 4 * zz, 4 * zz + 1, c, right)
            gather_push(a, 4 * zz, 4 * zz + 2, 1 - c if len(cs) == 2 else c, left)

    def forward(a, zz):
        got(a, 4 * zz + 1, 0)
        gather_push(a, 4 * zz + 1, 4 * zz + 3, 0, right)
        got(a, 4 * zz + 2, 1)
        gather_push(a, 4 * zz + 2, 4 * zz + 3, 1, left)

    kv_copies = []

    def project(p):
        rows = pl.ds(p * PAIR, PAIR)
        h = hid[rows]
        q[rows] = nn(h, wq[0]).astype(BF)
        kv[rows, pl.ds(0, WIDTH)] = nn(h, wq[1]).astype(BF)
        kv[rows, pl.ds(WIDTH, WIDTH)] = nn(h, wq[2]).astype(BF)
        kv_copies.append(
            push(kv.at[rows], kv.at[pl.ds(FRAME + p * PAIR, PAIR)], kvs_sem.at[p], kvr_sem.at[p], after)
        )

    for c in (0, 1):
        gather_push(0, 0, 4, c, across)
    spread(0, 0, (0, 1))
    loads[2].wait()
    forward(0, 0)
    spread(1, 0, (0, 1))
    loads[3].wait()
    got(0, 1, 1)
    project(0)
    got(0, 4, 0)
    spread(0, 1, (0,))
    got(0, 2, 0)
    got(0, 3, 0)
    got(0, 3, 1)
    project(1)
    got(0, 4, 1)
    spread(0, 1, (1,))
    for c in (0, 1):
        gather_push(1, 0, 4, c, across)
    forward(1, 0)
    forward(0, 1)
    got(0, 5, 1)
    project(2)
    got(1, 4, 0)
    spread(1, 1, (0,))
    got(0, 6, 0)
    got(0, 7, 0)
    got(0, 7, 1)
    project(3)
    got(1, 4, 1)
    spread(1, 1, (1,))
    loads[4].wait()

    def lanes(h):
        return pl.ds(pl.multiple_of(h * HEAD_DIM, HEAD_DIM), HEAD_DIM)

    def v_lanes(h):
        return pl.ds(pl.multiple_of(WIDTH + h * HEAD_DIM, HEAD_DIM), HEAD_DIM)

    acc_k[...] = jnp.zeros_like(acc_k)
    acc_v[...] = jnp.zeros_like(acc_v)
    for copy in kv_copies:
        copy.wait_recv()

    def turn(h, carry):
        kt[h] = kv[:, lanes(h)].astype(F32).T.astype(BF)
        return carry

    lax.fori_loop(0, HEADS_HERE, turn, 0)

    def score(i, carry):
        p = i // HEADS_HERE
        h = i - p * HEADS_HERE
        rows = pl.ds(pl.multiple_of(p * PAIR, PAIR), PAIR)
        qh = q[rows, lanes(h)]
        own = nt(kv[pl.ds(0, FRAME), lanes(h)], qh) * SCALE
        prev = nt(kv[pl.ds(FRAME, FRAME), lanes(h)], qh) * SCALE
        prev = jnp.where(tm > 0, prev, -1e30)
        top = jnp.maximum(jnp.max(own, axis=0, keepdims=True), jnp.max(prev, axis=0, keepdims=True))
        own = jnp.exp(own - top)
        prev = jnp.exp(prev - top)
        total = jnp.sum(own, axis=0, keepdims=True) + jnp.sum(prev, axis=0, keepdims=True)
        part_of = 1.0 / total
        probs[i, pl.ds(0, FRAME)] = own * part_of
        probs[i, pl.ds(FRAME, FRAME)] = prev * part_of
        return carry

    lax.fori_loop(0, 2 * HEADS_HERE, score, 0)
    forward(1, 1)
    lax.fori_loop(2 * HEADS_HERE, 4 * HEADS_HERE, score, 0)

    def backward(p):
        rows = pl.ds(p * PAIR, PAIR)
        ga_all = nt(cot[rows], wo[...]).astype(BF)
        ga_s[...] = ga_all

        def one(h, carry):
            ga = ga_s[:, lanes(h)]
            pt = probs[p * HEADS_HERE + h]
            dp = nt(kv[:, v_lanes(h)], ga)
            delta = jnp.sum(pt * dp, axis=0, keepdims=True)
            ds = (pt * (dp - delta) * SCALE).astype(BF)
            acc_k[:, lanes(h)] += nn(ds, q[rows, lanes(h)])
            acc_v[:, lanes(h)] += nn(pt.astype(BF), ga)
            g[rows, lanes(h)] = nn(kt[h], ds).T.astype(BF)
            return carry

        lax.fori_loop(0, HEADS_HERE, one, 0)

    got(1, 1, 1)
    backward(0)
    got(1, 2, 0)
    got(1, 3, 0)
    got(1, 3, 1)
    backward(1)
    got(1, 5, 1)
    backward(2)
    got(1, 6, 0)
    got(1, 7, 0)
    got(1, 7, 1)
    backward(3)

    backs = {}
    for zz in (1, 0):
        rows = pl.ds(zz * 256, 256)
        theirs = pl.ds(FRAME + zz * 256, 256)
        back_s[rows, pl.ds(0, WIDTH)] = acc_k[theirs].astype(BF)
        back_s[rows, pl.ds(WIDTH, WIDTH)] = acc_v[theirs].astype(BF)
        backs[zz] = push(back_s.at[rows], back_r.at[rows], bs_sem.at[zz], br_sem.at[zz], before)

    def join(zz):
        rows = pl.ds(zz * 256, 256)
        backs[zz].wait_recv()
        g[rows, pl.ds(WIDTH, WIDTH)] = (acc_k[rows] + back_r[rows, pl.ds(0, WIDTH)].astype(F32)).astype(BF)
        g[rows, pl.ds(2 * WIDTH, WIDTH)] = (acc_v[rows] + back_r[rows, pl.ds(WIDTH, WIDTH)].astype(F32)).astype(BF)

    def partials(zz, hf):
        def tile(n, carry):
            w_rows = pl.ds(pl.multiple_of(hf * COLS + n * 512, 512), 512)
            rows = pl.ds(zz * 256, 256)
            total = nt(g[rows, pl.ds(0, WIDTH)], wq[0, w_rows])
            total += nt(g[rows, pl.ds(WIDTH, WIDTH)], wq[1, w_rows])
            total += nt(g[rows, pl.ds(2 * WIDTH, WIDTH)], wq[2, w_rows])
            part[hf, rows, pl.ds(pl.multiple_of(n * 512, 512), 512)] = total.astype(BF)
            return carry

        lax.fori_loop(0, COLS // 512, tile, 0)

    sums = {}

    def sum_push(key, i, src, dst, peer):
        zz, hf = key
        k = (zz * 2 + hf) * 6 + i
        sums[key, i] = push(src, dst, rs_sem.at[k], rr_sem.at[k], peer)

    def opposite(zz, hf):
        u = zz * 2 + hf
        sum_push((zz, hf), 0, part.at[hf, chunk(4 * zz + 3, 0)], ra.at[u], right)
        sum_push((zz, hf), 1, part.at[hf, chunk(4 * zz + 3, 1)], rb.at[u], left)

    def singles(zz, hf):
        u = zz * 2 + hf
        sum_push((zz, hf), 2, part.at[hf, chunk(4 * zz + 2, 1)], rl.at[u, pl.ds(HALF, HALF)], right)
        sum_push((zz, hf), 3, part.at[hf, chunk(4 * zz + 1, 0)], rr.at[u, pl.ds(0, HALF)], left)

    def doubles(zz, hf):
        u = zz * 2 + hf
        to_right = chunk(4 * zz + 2, 0)
        to_left = chunk(4 * zz + 1, 1)
        sums[(zz, hf), 0].wait_recv()
        part[hf, to_right] = (part[hf, to_right].astype(F32) + ra[u].astype(F32)).astype(BF)
        sum_push((zz, hf), 4, part.at[hf, to_right], rl.at[u, pl.ds(0, HALF)], right)
        sums[(zz, hf), 1].wait_recv()
        part[hf, to_left] = (part[hf, to_left].astype(F32) + rb[u].astype(F32)).astype(BF)
        sum_push((zz, hf), 5, part.at[hf, to_left], rr.at[u, pl.ds(HALF, HALF)], left)

    crossing = {}

    def cross(hf):
        for i in (2, 3, 4, 5):
            sums[(1, hf), i].wait_recv()
        mine = part[hf, pl.ds(256, BLOCK)].astype(F32)
        zs[hf] = (mine + rl[2 + hf].astype(F32) + rr[2 + hf].astype(F32)).astype(BF)
        crossing[hf] = push(zs.at[hf], rz.at[hf], zs_sem.at[hf], zr_sem.at[hf], across)

    join(1)
    partials(1, 0)
    opposite(1, 0)
    singles(1, 0)
    partials(1, 1)
    opposite(1, 1)
    doubles(1, 0)
    singles(1, 1)
    join(0)
    partials(0, 0)
    opposite(0, 0)
    doubles(1, 1)
    cross(0)
    singles(0, 0)
    partials(0, 1)
    opposite(0, 1)
    doubles(0, 0)
    cross(1)
    singles(0, 1)
    doubles(0, 1)
    for hf in (0, 1):
        for i in (2, 3, 4, 5):
            sums[(0, hf), i].wait_recv()
    for hf in (0, 1):
        crossing[hf].wait_recv()

    for r in range(4):
        rows = pl.ds(r * 16, 16)
        scale = inv[rows, pl.ds(0, 1)]
        inner = jnp.zeros((16, 1), F32)
        for hf in (0, 1):
            cols = pl.ds(hf * COLS, COLS)
            total = (
                part[hf, rows].astype(F32) + rl[hf, rows].astype(F32) + rr[hf, rows].astype(F32)
                + rz[hf, rows].astype(F32)
            )
            total = total * gain[:, cols]
            inner += jnp.sum(total * (lat[rows, cols].astype(F32) * scale), axis=-1, keepdims=True)
            grad[rows, cols] = total
        inner = inner * (1.0 / D)
        normed = lat[rows].astype(F32) * scale
        out_ref[rows] = (cot[rows].astype(F32) + scale * (grad[rows] - normed * inner)).astype(BF)

    for copy in sent:
        copy.wait_send()


def shards(latents, cotangent, norm_gain, w_qkv, w_out):
    hbm = pl.BlockSpec(memory_space=pl.ANY)
    dma = pltpu.SemaphoreType.DMA
    return pl.pallas_call(
        kernel,
        out_shape=jax.ShapeDtypeStruct((BLOCK, D), BF),
        in_specs=[hbm] * 5,
        out_specs=pl.BlockSpec(memory_space=pltpu.VMEM),
        scratch_shapes=[
            pltpu.VMEM((BLOCK, D), BF),
            pltpu.VMEM((1, D), F32),
            pltpu.VMEM((3, D, WIDTH), BF),
            pltpu.VMEM((WIDTH, D), BF),
            pltpu.VMEM((FRAME, D), BF),
            pltpu.VMEM((FRAME, D), BF),
            pltpu.VMEM((BLOCK, 128), F32),
            pltpu.VMEM((FRAME, WIDTH), BF),
            pltpu.VMEM((2 * FRAME, 2 * WIDTH), BF),
            pltpu.VMEM((HEADS_HERE, HEAD_DIM, 2 * FRAME), BF),
            pltpu.VMEM((4 * HEADS_HERE, 2 * FRAME, PAIR), F32),
            pltpu.VMEM((2 * FRAME, WIDTH), F32),
            pltpu.VMEM((2 * FRAME, WIDTH), F32),
            pltpu.VMEM((FRAME, 2 * WIDTH), BF),
            pltpu.VMEM((FRAME, 2 * WIDTH), BF),
            pltpu.VMEM((FRAME, 3 * WIDTH), BF),
            pltpu.VMEM((2, FRAME, COLS), BF),
            pltpu.VMEM((4, HALF, COLS), BF),
            pltpu.VMEM((4, HALF, COLS), BF),
            pltpu.VMEM((4, BLOCK, COLS), BF),
            pltpu.VMEM((4, BLOCK, COLS), BF),
            pltpu.VMEM((2, BLOCK, COLS), BF),
            pltpu.VMEM((2, BLOCK, COLS), BF),
            pltpu.VMEM((PAIR, WIDTH), BF),
            pltpu.VMEM((BLOCK, D), F32),
            dma((5,)),
            dma((2, 16)),
            dma((2, 16)),
            dma((4,)),
            dma((4,)),
            dma((2,)),
            dma((2,)),
            dma((24,)),
            dma((24,)),
            dma((2,)),
            dma((2,)),
        ],
        compiler_params=pltpu.CompilerParams(
            collective_id=0, has_side_effects=True, vmem_limit_bytes=56 * 1024 * 1024
        ),
        name="frame_attention_grad",
    )(latents, cotangent, norm_gain.reshape(1, D), jnp.transpose(w_qkv, (1, 0, 2)), w_out)


def solution(mesh):
    return jax.shard_map(
        shards,
        mesh=mesh,
        in_specs=(
            P(("tm", "head"), None),
            P(("tm", "head"), None),
            P(),
            P(None, None, "head"),
            P("head", None),
        ),
        out_specs=P(("tm", "head"), None),
        check_vma=False,
    )
```

time: 348 us -> 112 us (0.32)
  waiting for transfers between devices: 270 us -> 0 us
  Pallas kernels: 0 us -> 110 us
  matrix products: 29.6 us -> 0 us
  between operations: 13.4 us -> 0.01 us
  local copies, waits for them, and re-layouts: 14.6 us -> 1.77 us
  starting transfers between devices: 10.3 us -> 0 us
  other arithmetic: 9.7 us -> 0 us
    all_gather x2 -> x0, waiting for transfers between devices: 158 us -> none  [the longest x1 84.3 us: shards(): lax.all_gather(hidden, 'head', axis=0, tiled=True)]
    pallas_call x0 -> x1, Pallas kernels: none -> 110 us  [shards(): pl.pallas_call(kernel, out_shape=jax.ShapeDtypeStruct((BLOCK, D), BF), in...]
    reduce_scatter x1 -> x0, waiting for transfers between devices: 107 us -> none  [shards(): lax.psum_scatter(lax.dot_general(grad_qkv, flat_w, (((1,), (1,)), ((), ()...]
    dot_general x13 -> x0, matrix products: 29.6 us -> none  [the longest x1 8.22 us: shards(): jnp.dot(lax.all_gather(hidden, 'head', axis=0, tiled=True), flat_w, prefe...]
    ppermute x4 -> x0, starting transfers between devices: 10.3 us -> none  [from_behind(): return lax.ppermute(block, axis, route)]
    unnamed x19 -> x1, local copies, waits for them, and re-layouts: 10.3 us -> 1.77 us
    convert_element_type x3 -> x0, other arithmetic: 5.93 us -> none  [the longest x1 2.03 us: shards(): return result.astype(jnp.bfloat16)]
    ppermute x4 -> x0, waiting for transfers between devices: 4.71 us -> none  [from_behind(): return lax.ppermute(block, axis, route)]
  transfers between devices with their start and end apart: 7 -> 0, of which waited for: 4 -> 0; matrix products, arithmetic and copies ran while one was open for 12% -> 0% of each run, Pallas kernels for 0% -> 0%
where the time goes in v1:
time: 112 us
  Pallas kernels  110 us (98%)
  local copies, waits for them, and re-layouts  1.77 us (2%)
    pallas_call x1, Pallas kernels, shards(): pl.pallas_call(kernel, out_shape=jax.ShapeDtypeStruct((BLOCK, D), BF), in...  110 us

profile of v1, /device:TPU:1, one launch (start us, length us, event | category | flops | bytes accessed | tf_op | source)
XLA Modules:
  0.0 112.2 jit_solution(6058374120826430017)
XLA Ops:
  0.0 110.5 %frame_attention_grad.1 = bf16[64,3072]{1,0:T(8,128)(2,1)} custom-call(bf16[64,3072]{1,0:T(8,128)(2,1)} %lat_h.1, bf16[64,3072]{1,0:T(8,128)(2,1)} %cot_h.1, f32[1,3072]{1,0:T(1,128)} %bitcast.3, bf16[3,3072,384]{2,1,0:T(8,128)(2,1)} %bitcast.2, bf16[384,3072]{1,0:T(8,128)(2,1)} %wout_h.1), custom_call_target="tpu_custom_call" | custom-call | tf_op jit(solution)/shard_map/frame_attention_grad/pallas_call | solution.py:338
  110.5 1.8 %copy.7 = bf16[64,3072]{1,0:T(8,128)(2,1)} copy(bf16[64,3072]{1,0:T(8,128)(2,1)} %frame_attention_grad.1) | data formatting | bytes 786432

commit v2 on v1

--- a/solution.py
+++ b/solution.py
@@ -36,7 +36,7 @@
 def kernel(
     lat_h, cot_h, gain_h, wqkv_h, wout_h, out_ref,
     lat, gain, wq, wo, hid, cot, inv, q, kv, kt, probs, acc_k, acc_v, back_s, back_r, g,
-    part, ra, rb, rl, rr, zs, rz, ga_s, grad,
+    part, ra, rb, rl, rr, zs, rz, ga_s, ds_s, grad,
     ld_sem, gs_sem, gr_sem, kvs_sem, kvr_sem, bs_sem, br_sem, rs_sem, rr_sem, zs_sem, zr_sem,
 ):
     tm = lax.axis_index("tm")
@@ -102,11 +102,17 @@
             gather_push(a, 4 * zz, 4 * zz + 1, c, right)
             gather_push(a, 4 * zz, 4 * zz + 2, 1 - c if len(cs) == 2 else c, left)
 
-    def forward(a, zz):
+    def forward_right(a, zz):
         got(a, 4 * zz + 1, 0)
         gather_push(a, 4 * zz + 1, 4 * zz + 3, 0, right)
+
+    def forward_left(a, zz):
         got(a, 4 * zz + 2, 1)
         gather_push(a, 4 * zz + 2, 4 * zz + 3, 1, left)
+
+    def forward(a, zz):
+        forward_right(a, zz)
+        forward_left(a, zz)
 
     kv_copies = []
 
@@ -125,7 +131,8 @@
     spread(0, 0, (0, 1))
     loads[2].wait()
     forward(0, 0)
-    spread(1, 0, (0, 1))
+    gather_push(1, 0, 1, 0, right)
+    gather_push(1, 0, 2, 1, left)
     loads[3].wait()
     got(0, 1, 1)
     project(0)
@@ -139,18 +146,18 @@
     spread(0, 1, (1,))
     for c in (0, 1):
         gather_push(1, 0, 4, c, across)
-    forward(1, 0)
     forward(0, 1)
+    gather_push(1, 0, 1, 1, right)
+    gather_push(1, 0, 2, 0, left)
     got(0, 5, 1)
     project(2)
+    forward(1, 0)
     got(1, 4, 0)
     spread(1, 1, (0,))
     got(0, 6, 0)
     got(0, 7, 0)
     got(0, 7, 1)
     project(3)
-    got(1, 4, 1)
-    spread(1, 1, (1,))
     loads[4].wait()
 
     def lanes(h):
@@ -188,29 +195,33 @@
         return carry
 
     lax.fori_loop(0, 2 * HEADS_HERE, score, 0)
-    forward(1, 1)
+    got(1, 4, 1)
+    spread(1, 1, (1,))
     lax.fori_loop(2 * HEADS_HERE, 4 * HEADS_HERE, score, 0)
+
+    def score_grads(p, h):
+        pt = probs[p * HEADS_HERE + h]
+        dp = nt(kv[:, v_lanes(h)], ga_s[:, lanes(h)])
+        delta = jnp.sum(pt * dp, axis=0, keepdims=True)
+        return pt, (pt * (dp - delta) * SCALE).astype(BF)
 
     def backward(p):
         rows = pl.ds(p * PAIR, PAIR)
-        ga_all = nt(cot[rows], wo[...]).astype(BF)
-        ga_s[...] = ga_all
+        ga_s[...] = nt(cot[rows], wo[...]).astype(BF)
 
         def one(h, carry):
-            ga = ga_s[:, lanes(h)]
-            pt = probs[p * HEADS_HERE + h]
-            dp = nt(kv[:, v_lanes(h)], ga)
-            delta = jnp.sum(pt * dp, axis=0, keepdims=True)
-            ds = (pt * (dp - delta) * SCALE).astype(BF)
+            pt, ds = score_grads(p, h)
             acc_k[:, lanes(h)] += nn(ds, q[rows, lanes(h)])
-            acc_v[:, lanes(h)] += nn(pt.astype(BF), ga)
+            acc_v[:, lanes(h)] += nn(pt.astype(BF), ga_s[:, lanes(h)])
             g[rows, lanes(h)] = nn(kt[h], ds).T.astype(BF)
             return carry
 
         lax.fori_loop(0, HEADS_HERE, one, 0)
 
+    forward_right(1, 1)
     got(1, 1, 1)
     backward(0)
+    forward_left(1, 1)
     got(1, 2, 0)
     got(1, 3, 0)
     got(1, 3, 1)
@@ -220,26 +231,45 @@
     got(1, 6, 0)
     got(1, 7, 0)
     got(1, 7, 1)
-    backward(3)
-
-    backs = {}
-    for zz in (1, 0):
-        rows = pl.ds(zz * 256, 256)
-        theirs = pl.ds(FRAME + zz * 256, 256)
-        back_s[rows, pl.ds(0, WIDTH)] = acc_k[theirs].astype(BF)
-        back_s[rows, pl.ds(WIDTH, WIDTH)] = acc_v[theirs].astype(BF)
-        backs[zz] = push(back_s.at[rows], back_r.at[rows], bs_sem.at[zz], br_sem.at[zz], before)
-
-    def join(zz):
-        rows = pl.ds(zz * 256, 256)
-        backs[zz].wait_recv()
+
+    last = pl.ds(3 * PAIR, PAIR)
+    own = pl.ds(0, FRAME)
+    prev = pl.ds(FRAME, FRAME)
+    ga_s[...] = nt(cot[last], wo[...]).astype(BF)
+
+    def last_prev(h, carry):
+        pt, ds = score_grads(3, h)
+        ds_s[h] = ds
+        back_s[:, lanes(h)] = (acc_k[prev, lanes(h)] + nn(ds[FRAME:], q[last, lanes(h)])).astype(BF)
+        back_s[:, v_lanes(h)] = (acc_v[prev, lanes(h)] + nn(pt[FRAME:].astype(BF), ga_s[:, lanes(h)])).astype(BF)
+        return carry
+
+    lax.fori_loop(0, HEADS_HERE, last_prev, 0)
+    pieces = ((448, 64), (256, 192), (0, 256))
+    backs = []
+    for i, (start, size) in enumerate(pieces):
+        rows = pl.ds(start, size)
+        backs.append(push(back_s.at[rows], back_r.at[rows], bs_sem.at[i], br_sem.at[i], before))
+
+    def last_own(h, carry):
+        g[last, lanes(h)] = nn(kt[h], ds_s[h]).T.astype(BF)
+        acc_k[own, lanes(h)] += nn(ds_s[h, own], q[last, lanes(h)])
+        acc_v[own, lanes(h)] += nn(probs[3 * HEADS_HERE + h, own].astype(BF), ga_s[:, lanes(h)])
+        return carry
+
+    lax.fori_loop(0, HEADS_HERE, last_own, 0)
+
+    def join(i):
+        rows = pl.ds(*pieces[i])
+        backs[i].wait_recv()
         g[rows, pl.ds(WIDTH, WIDTH)] = (acc_k[rows] + back_r[rows, pl.ds(0, WIDTH)].astype(F32)).astype(BF)
         g[rows, pl.ds(2 * WIDTH, WIDTH)] = (acc_v[rows] + back_r[rows, pl.ds(WIDTH, WIDTH)].astype(F32)).astype(BF)
 
-    def partials(zz, hf):
+    def partials(i, hf):
+        rows = pl.ds(*pieces[i])
+
         def tile(n, carry):
             w_rows = pl.ds(pl.multiple_of(hf * COLS + n * 512, 512), 512)
-            rows = pl.ds(zz * 256, 256)
             total = nt(g[rows, pl.ds(0, WIDTH)], wq[0, w_rows])
             total += nt(g[rows, pl.ds(WIDTH, WIDTH)], wq[1, w_rows])
             total += nt(g[rows, pl.ds(2 * WIDTH, WIDTH)], wq[2, w_rows])
@@ -285,21 +315,24 @@
         zs[hf] = (mine + rl[2 + hf].astype(F32) + rr[2 + hf].astype(F32)).astype(BF)
         crossing[hf] = push(zs.at[hf], rz.at[hf], zs_sem.at[hf], zr_sem.at[hf], across)
 
+    join(0)
+    partials(0, 0)
+    opposite(1, 0)
+    partials(0, 1)
+    opposite(1, 1)
     join(1)
     partials(1, 0)
-    opposite(1, 0)
     singles(1, 0)
+    doubles(1, 0)
     partials(1, 1)
-    opposite(1, 1)
-    doubles(1, 0)
     singles(1, 1)
-    join(0)
-    partials(0, 0)
+    doubles(1, 1)
+    join(2)
+    partials(2, 0)
     opposite(0, 0)
-    doubles(1, 1)
+    singles(0, 0)
     cross(0)
-    singles(0, 0)
-    partials(0, 1)
+    partials(2, 1)
     opposite(0, 1)
     doubles(0, 0)
     cross(1)
@@ -365,14 +398,15 @@
             pltpu.VMEM((2, BLOCK, COLS), BF),
             pltpu.VMEM((2, BLOCK, COLS), BF),
             pltpu.VMEM((PAIR, WIDTH), BF),
+            pltpu.VMEM((HEADS_HERE, 2 * FRAME, PAIR), BF),
             pltpu.VMEM((BLOCK, D), F32),
             dma((5,)),
             dma((2, 16)),
             dma((2, 16)),
             dma((4,)),
             dma((4,)),
-            dma((2,)),
-            dma((2,)),
+            dma((3,)),
+            dma((3,)),
             dma((24,)),
             dma((24,)),
             dma((2,)),

time: 112 us -> 111 us (level)
    pallas_call x1, Pallas kernels: 110 us -> 109 us  [shards(): pl.pallas_call(kernel, out_shape=jax.ShapeDtypeStruct((BLOCK, D), BF), in...]
where the time goes in v2:
time: 111 us
  Pallas kernels  109 us (98%)
  local copies, waits for them, and re-layouts  1.77 us (2%)
    pallas_call x1, Pallas kernels, shards(): pl.pallas_call(kernel, out_shape=jax.ShapeDtypeStruct((BLOCK, D), BF), in...  109 us

profile of v2, /device:TPU:1, one launch (start us, length us, event | category | flops | bytes accessed | tf_op | source)
XLA Modules:
  0.0 111.0 jit_solution(11690843798036663779)
XLA Ops:
  0.0 109.2 %frame_attention_grad.1 = bf16[64,3072]{1,0:T(8,128)(2,1)} custom-call(bf16[64,3072]{1,0:T(8,128)(2,1)} %lat_h.1, bf16[64,3072]{1,0:T(8,128)(2,1)} %cot_h.1, f32[1,3072]{1,0:T(1,128)} %bitcast.3, bf16[3,3072,384]{2,1,0:T(8,128)(2,1)} %bitcast.2, bf16[384,3072]{1,0:T(8,128)(2,1)} %wout_h.1), custom_call_target="tpu_custom_call" | custom-call | tf_op jit(solution)/shard_map/frame_attention_grad/pallas_call | solution.py:371
  109.2 1.8 %copy.7 = bf16[64,3072]{1,0:T(8,128)(2,1)} copy(bf16[64,3072]{1,0:T(8,128)(2,1)} %frame_attention_grad.1) | data formatting | bytes 786432

commit v3 on v2

--- a/solution.py
+++ b/solution.py
@@ -15,9 +15,11 @@
 WIDTH = HEADS_HERE * HEAD_DIM
 BLOCK = 64
 HALF = BLOCK // 2
+STEP = BLOCK // 4
 FRAME = 512
 PAIR = 2 * BLOCK
-COLS = D // 2
+PARTS = 4
+COLS = D // PARTS
 N_TM = 32
 X = 4
 SCALE = HEAD_DIM ** (-0.5)
@@ -36,7 +38,7 @@
 def kernel(
     lat_h, cot_h, gain_h, wqkv_h, wout_h, out_ref,
     lat, gain, wq, wo, hid, cot, inv, q, kv, kt, probs, acc_k, acc_v, back_s, back_r, g,
-    part, ra, rb, rl, rr, zs, rz, ga_s, ds_s, grad,
+    part, ra, rb, rl, rr, zs, rz, ga_s, ds_s, ga_f, ds_f, pb_f, grad,
     ld_sem, gs_sem, gr_sem, kvs_sem, kvr_sem, bs_sem, br_sem, rs_sem, rr_sem, zs_sem, zr_sem,
 ):
     tm = lax.axis_index("tm")
@@ -89,30 +91,31 @@
     moves = {}
 
     def gather_push(a, src_slot, dst_slot, c, peer):
-        i = dst_slot * 2 + c
+        i = dst_slot * 4 + c
         moves[a, dst_slot, c] = push(
-            bufs[a].at[chunk(src_slot, c)], bufs[a].at[chunk(dst_slot, c)], gs_sem.at[a, i], gr_sem.at[a, i], peer
+            bufs[a].at[pl.ds(src_slot * BLOCK + c * STEP, STEP)], bufs[a].at[pl.ds(dst_slot * BLOCK + c * STEP, STEP)],
+            gs_sem.at[a, i], gr_sem.at[a, i], peer,
         )
 
-    def got(a, slot, c):
-        moves[a, slot, c].wait_recv()
-
-    def spread(a, zz, cs):
+    def got(a, slot, cs=(0, 1, 2, 3)):
         for c in cs:
-            gather_push(a, 4 * zz, 4 * zz + 1, c, right)
-            gather_push(a, 4 * zz, 4 * zz + 2, 1 - c if len(cs) == 2 else c, left)
-
-    def forward_right(a, zz):
-        got(a, 4 * zz + 1, 0)
-        gather_push(a, 4 * zz + 1, 4 * zz + 3, 0, right)
-
-    def forward_left(a, zz):
-        got(a, 4 * zz + 2, 1)
-        gather_push(a, 4 * zz + 2, 4 * zz + 3, 1, left)
-
-    def forward(a, zz):
-        forward_right(a, zz)
-        forward_left(a, zz)
+            moves[a, slot, c].wait_recv()
+
+    def to_right(a, zz, c):
+        gather_push(a, 4 * zz, 4 * zz + 1, c, right)
+
+    def to_left(a, zz, c):
+        gather_push(a, 4 * zz, 4 * zz + 2, c, left)
+
+    def spread(a, c):
+        got(a, 4, (c,))
+        to_right(a, 1, c)
+        to_left(a, 1, c)
+
+    def forward(a, zz, c):
+        near = 4 * zz + 1 + c % 2
+        got(a, near, (c,))
+        gather_push(a, near, 4 * zz + 3, c, left if c % 2 else right)
 
     kv_copies = []
 
@@ -126,38 +129,39 @@
             push(kv.at[rows], kv.at[pl.ds(FRAME + p * PAIR, PAIR)], kvs_sem.at[p], kvr_sem.at[p], after)
         )
 
-    for c in (0, 1):
+    for c in range(4):
         gather_push(0, 0, 4, c, across)
-    spread(0, 0, (0, 1))
+        to_right(0, 0, (0, 2, 1, 3)[c])
+        to_left(0, 0, (1, 3, 0, 2)[c])
     loads[2].wait()
-    forward(0, 0)
-    gather_push(1, 0, 1, 0, right)
-    gather_push(1, 0, 2, 1, left)
+    for c in range(4):
+        forward(0, 0, c)
+        (to_left if c % 2 else to_right)(1, 0, c)
     loads[3].wait()
-    got(0, 1, 1)
+    got(0, 1, (1, 3))
     project(0)
-    got(0, 4, 0)
-    spread(0, 1, (0,))
-    got(0, 2, 0)
-    got(0, 3, 0)
-    got(0, 3, 1)
+    spread(0, 0)
+    spread(0, 1)
+    got(0, 2, (0, 2))
+    got(0, 3)
     project(1)
-    got(0, 4, 1)
-    spread(0, 1, (1,))
-    for c in (0, 1):
+    spread(0, 2)
+    for c in range(4):
         gather_push(1, 0, 4, c, across)
-    forward(0, 1)
-    gather_push(1, 0, 1, 1, right)
-    gather_push(1, 0, 2, 0, left)
-    got(0, 5, 1)
+    spread(0, 3)
+    for c in range(4):
+        forward(0, 1, c)
+    for c in range(4):
+        (to_right if c % 2 else to_left)(1, 0, c)
+    got(0, 5, (1, 3))
     project(2)
-    forward(1, 0)
-    got(1, 4, 0)
-    spread(1, 1, (0,))
-    got(0, 6, 0)
-    got(0, 7, 0)
-    got(0, 7, 1)
+    for c in range(4):
+        forward(1, 0, c)
+    spread(1, 0)
+    got(0, 6, (0, 2))
+    got(0, 7)
     project(3)
+    spread(1, 1)
     loads[4].wait()
 
     def lanes(h):
@@ -166,8 +170,6 @@
     def v_lanes(h):
         return pl.ds(pl.multiple_of(WIDTH + h * HEAD_DIM, HEAD_DIM), HEAD_DIM)
 
-    acc_k[...] = jnp.zeros_like(acc_k)
-    acc_v[...] = jnp.zeros_like(acc_v)
     for copy in kv_copies:
         copy.wait_recv()
 
@@ -195,8 +197,9 @@
         return carry
 
     lax.fori_loop(0, 2 * HEADS_HERE, score, 0)
-    got(1, 4, 1)
-    spread(1, 1, (1,))
+    spread(1, 2)
+    forward(1, 1, 0)
+    forward(1, 1, 1)
     lax.fori_loop(2 * HEADS_HERE, 4 * HEADS_HERE, score, 0)
 
     def score_grads(p, h):
@@ -218,19 +221,38 @@
 
         lax.fori_loop(0, HEADS_HERE, one, 0)
 
-    forward_right(1, 1)
-    got(1, 1, 1)
-    backward(0)
-    forward_left(1, 1)
-    got(1, 2, 0)
-    got(1, 3, 0)
-    got(1, 3, 1)
-    backward(1)
-    got(1, 5, 1)
+
+    def backward_first():
+        for p in (0, 1):
+            ga_f[pl.ds(p * PAIR, PAIR)] = nt(cot[pl.ds(p * PAIR, PAIR)], wo[...]).astype(BF)
+
+        def one(h, carry):
+            rows = pl.ds(0, 2 * PAIR)
+            dp = nt(kv[:, v_lanes(h)], ga_f[:, lanes(h)])
+            for p in (0, 1):
+                pt = probs[p * HEADS_HERE + h]
+                dpp = dp[:, p * PAIR : (p + 1) * PAIR]
+                delta = jnp.sum(pt * dpp, axis=0, keepdims=True)
+                ds_f[:, pl.ds(p * PAIR, PAIR)] = (pt * (dpp - delta) * SCALE).astype(BF)
+                pb_f[:, pl.ds(p * PAIR, PAIR)] = pt.astype(BF)
+            acc_k[:, lanes(h)] = nn(ds_f[...], q[rows, lanes(h)])
+            acc_v[:, lanes(h)] = nn(pb_f[...], ga_f[:, lanes(h)])
+            g[rows, lanes(h)] = nn(kt[h], ds_f[...]).T.astype(BF)
+            return carry
+
+        lax.fori_loop(0, HEADS_HERE, one, 0)
+
+    spread(1, 3)
+    got(1, 1, (1, 3))
+    got(1, 2, (0, 2))
+    got(1, 3)
+    backward_first()
+    forward(1, 1, 2)
+    forward(1, 1, 3)
+    got(1, 5, (1, 3))
     backward(2)
-    got(1, 6, 0)
-    got(1, 7, 0)
-    got(1, 7, 1)
+    got(1, 6, (0, 2))
+    got(1, 7)
 
     last = pl.ds(3 * PAIR, PAIR)
     own = pl.ds(0, FRAME)
@@ -269,42 +291,42 @@
         rows = pl.ds(*pieces[i])
 
         def tile(n, carry):
-            w_rows = pl.ds(pl.multiple_of(hf * COLS + n * 512, 512), 512)
+            w_rows = pl.ds(pl.multiple_of(hf * COLS + n * 384, 128), 384)
             total = nt(g[rows, pl.ds(0, WIDTH)], wq[0, w_rows])
             total += nt(g[rows, pl.ds(WIDTH, WIDTH)], wq[1, w_rows])
             total += nt(g[rows, pl.ds(2 * WIDTH, WIDTH)], wq[2, w_rows])
-            part[hf, rows, pl.ds(pl.multiple_of(n * 512, 512), 512)] = total.astype(BF)
+            part[hf, rows, pl.ds(pl.multiple_of(n * 384, 128), 384)] = total.astype(BF)
             return carry
 
-        lax.fori_loop(0, COLS // 512, tile, 0)
+        lax.fori_loop(0, COLS // 384, tile, 0)
 
     sums = {}
 
     def sum_push(key, i, src, dst, peer):
         zz, hf = key
-        k = (zz * 2 + hf) * 6 + i
+        k = (zz * PARTS + hf) * 6 + i
         sums[key, i] = push(src, dst, rs_sem.at[k], rr_sem.at[k], peer)
 
     def opposite(zz, hf):
-        u = zz * 2 + hf
+        u = zz * PARTS + hf
         sum_push((zz, hf), 0, part.at[hf, chunk(4 * zz + 3, 0)], ra.at[u], right)
         sum_push((zz, hf), 1, part.at[hf, chunk(4 * zz + 3, 1)], rb.at[u], left)
 
     def singles(zz, hf):
-        u = zz * 2 + hf
+        u = zz * PARTS + hf
         sum_push((zz, hf), 2, part.at[hf, chunk(4 * zz + 2, 1)], rl.at[u, pl.ds(HALF, HALF)], right)
         sum_push((zz, hf), 3, part.at[hf, chunk(4 * zz + 1, 0)], rr.at[u, pl.ds(0, HALF)], left)
 
     def doubles(zz, hf):
-        u = zz * 2 + hf
-        to_right = chunk(4 * zz + 2, 0)
-        to_left = chunk(4 * zz + 1, 1)
+        u = zz * PARTS + hf
+        for_right = chunk(4 * zz + 2, 0)
+        for_left = chunk(4 * zz + 1, 1)
         sums[(zz, hf), 0].wait_recv()
-        part[hf, to_right] = (part[hf, to_right].astype(F32) + ra[u].astype(F32)).astype(BF)
-        sum_push((zz, hf), 4, part.at[hf, to_right], rl.at[u, pl.ds(0, HALF)], right)
+        part[hf, for_right] = (part[hf, for_right].astype(F32) + ra[u].astype(F32)).astype(BF)
+        sum_push((zz, hf), 4, part.at[hf, for_right], rl.at[u, pl.ds(0, HALF)], right)
         sums[(zz, hf), 1].wait_recv()
-        part[hf, to_left] = (part[hf, to_left].astype(F32) + rb[u].astype(F32)).astype(BF)
-        sum_push((zz, hf), 5, part.at[hf, to_left], rr.at[u, pl.ds(HALF, HALF)], left)
+        part[hf, for_left] = (part[hf, for_left].astype(F32) + rb[u].astype(F32)).astype(BF)
+        sum_push((zz, hf), 5, part.at[hf, for_left], rr.at[u, pl.ds(HALF, HALF)], left)
 
     crossing = {}
 
@@ -312,43 +334,41 @@
         for i in (2, 3, 4, 5):
             sums[(1, hf), i].wait_recv()
         mine = part[hf, pl.ds(256, BLOCK)].astype(F32)
-        zs[hf] = (mine + rl[2 + hf].astype(F32) + rr[2 + hf].astype(F32)).astype(BF)
+        zs[hf] = (mine + rl[PARTS + hf].astype(F32) + rr[PARTS + hf].astype(F32)).astype(BF)
         crossing[hf] = push(zs.at[hf], rz.at[hf], zs_sem.at[hf], zr_sem.at[hf], across)
 
     join(0)
-    partials(0, 0)
-    opposite(1, 0)
-    partials(0, 1)
-    opposite(1, 1)
+    for hf in range(PARTS):
+        partials(0, hf)
+        opposite(1, hf)
     join(1)
-    partials(1, 0)
-    singles(1, 0)
-    doubles(1, 0)
-    partials(1, 1)
-    singles(1, 1)
-    doubles(1, 1)
+    for hf in range(PARTS):
+        partials(1, hf)
+        singles(1, hf)
+        doubles(1, hf)
+        if hf:
+            cross(hf - 1)
     join(2)
-    partials(2, 0)
-    opposite(0, 0)
-    singles(0, 0)
-    cross(0)
-    partials(2, 1)
-    opposite(0, 1)
-    doubles(0, 0)
-    cross(1)
-    singles(0, 1)
-    doubles(0, 1)
-    for hf in (0, 1):
+    for hf in range(PARTS):
+        partials(2, hf)
+        opposite(0, hf)
+        singles(0, hf)
+        if hf:
+            doubles(0, hf - 1)
+        else:
+            cross(PARTS - 1)
+    doubles(0, PARTS - 1)
+    for hf in range(PARTS):
         for i in (2, 3, 4, 5):
             sums[(0, hf), i].wait_recv()
-    for hf in (0, 1):
+    for hf in range(PARTS):
         crossing[hf].wait_recv()
 
     for r in range(4):
         rows = pl.ds(r * 16, 16)
         scale = inv[rows, pl.ds(0, 1)]
         inner = jnp.zeros((16, 1), F32)
-        for hf in (0, 1):
+        for hf in range(PARTS):
             cols = pl.ds(hf * COLS, COLS)
             total = (
                 part[hf, rows].astype(F32) + rl[hf, rows].astype(F32) + rr[hf, rows].astype(F32)
@@ -390,27 +410,30 @@
             pltpu.VMEM((FRAME, 2 * WIDTH), BF),
             pltpu.VMEM((FRAME, 2 * WIDTH), BF),
             pltpu.VMEM((FRAME, 3 * WIDTH), BF),
-            pltpu.VMEM((2, FRAME, COLS), BF),
-            pltpu.VMEM((4, HALF, COLS), BF),
-            pltpu.VMEM((4, HALF, COLS), BF),
-            pltpu.VMEM((4, BLOCK, COLS), BF),
-            pltpu.VMEM((4, BLOCK, COLS), BF),
-            pltpu.VMEM((2, BLOCK, COLS), BF),
-            pltpu.VMEM((2, BLOCK, COLS), BF),
+            pltpu.VMEM((PARTS, FRAME, COLS), BF),
+            pltpu.VMEM((2 * PARTS, HALF, COLS), BF),
+            pltpu.VMEM((2 * PARTS, HALF, COLS), BF),
+            pltpu.VMEM((2 * PARTS, BLOCK, COLS), BF),
+            pltpu.VMEM((2 * PARTS, BLOCK, COLS), BF),
+            pltpu.VMEM((PARTS, BLOCK, COLS), BF),
+            pltpu.VMEM((PARTS, BLOCK, COLS), BF),
             pltpu.VMEM((PAIR, WIDTH), BF),
             pltpu.VMEM((HEADS_HERE, 2 * FRAME, PAIR), BF),
+            pltpu.VMEM((2 * PAIR, WIDTH), BF),
+            pltpu.VMEM((2 * FRAME, 2 * PAIR), BF),
+            pltpu.VMEM((2 * FRAME, 2 * PAIR), BF),
             pltpu.VMEM((BLOCK, D), F32),
             dma((5,)),
-            dma((2, 16)),
-            dma((2, 16)),
+            dma((2, 32)),
+            dma((2, 32)),
             dma((4,)),
             dma((4,)),
             dma((3,)),
             dma((3,)),
-            dma((24,)),
-            dma((24,)),
-            dma((2,)),
-            dma((2,)),
+            dma((12 * PARTS,)),
+            dma((12 * PARTS,)),
+            dma((PARTS,)),
+            dma((PARTS,)),
         ],
         compiler_params=pltpu.CompilerParams(
             collective_id=0, has_side_effects=True, vmem_limit_bytes=56 * 1024 * 1024

time: 111 us -> 110 us (level)
    pallas_call x1, Pallas kernels: 109 us -> 108 us  [shards(): pl.pallas_call(kernel, out_shape=jax.ShapeDtypeStruct((BLOCK, D), BF), in...]
where the time goes in v3:
time: 110 us
  Pallas kernels  108 us (98%)
  local copies, waits for them, and re-layouts  1.77 us (2%)
    pallas_call x1, Pallas kernels, shards(): pl.pallas_call(kernel, out_shape=jax.ShapeDtypeStruct((BLOCK, D), BF), in...  108 us

profile of v3, /device:TPU:1, one launch (start us, length us, event | category | flops | bytes accessed | tf_op | source)
XLA Modules:
  0.0 109.7 jit_solution(6514419532832540730)
XLA Ops:
  0.0 108.0 %frame_attention_grad.1 = bf16[64,3072]{1,0:T(8,128)(2,1)} custom-call(bf16[64,3072]{1,0:T(8,128)(2,1)} %lat_h.1, bf16[64,3072]{1,0:T(8,128)(2,1)} %cot_h.1, f32[1,3072]{1,0:T(1,128)} %bitcast.3, bf16[3,3072,384]{2,1,0:T(8,128)(2,1)} %bitcast.2, bf16[384,3072]{1,0:T(8,128)(2,1)} %wout_h.1), custom_call_target="tpu_custom_call" | custom-call | tf_op jit(solution)/shard_map/frame_attention_grad/pallas_call | solution.py:391
  108.0 1.8 %copy.7 = bf16[64,3072]{1,0:T(8,128)(2,1)} copy(bf16[64,3072]{1,0:T(8,128)(2,1)} %frame_attention_grad.1) | data formatting | bytes 786432

commit v4 on v3

--- a/solution.py
+++ b/solution.py
@@ -136,7 +136,8 @@
     loads[2].wait()
     for c in range(4):
         forward(0, 0, c)
-        (to_left if c % 2 else to_right)(1, 0, c)
+        to_right(1, 0, (0, 2, 1, 3)[c])
+        to_left(1, 0, (1, 3, 0, 2)[c])
     loads[3].wait()
     got(0, 1, (1, 3))
     project(0)
@@ -145,18 +146,16 @@
     got(0, 2, (0, 2))
     got(0, 3)
     project(1)
+    for c in range(4):
+        forward(1, 0, c)
     spread(0, 2)
     for c in range(4):
         gather_push(1, 0, 4, c, across)
     spread(0, 3)
     for c in range(4):
         forward(0, 1, c)
-    for c in range(4):
-        (to_right if c % 2 else to_left)(1, 0, c)
     got(0, 5, (1, 3))
     project(2)
-    for c in range(4):
-        forward(1, 0, c)
     spread(1, 0)
     got(0, 6, (0, 2))
     got(0, 7)
@@ -346,18 +345,14 @@
         partials(1, hf)
         singles(1, hf)
         doubles(1, hf)
-        if hf:
-            cross(hf - 1)
     join(2)
     for hf in range(PARTS):
         partials(2, hf)
         opposite(0, hf)
         singles(0, hf)
-        if hf:
-            doubles(0, hf - 1)
-        else:
-            cross(PARTS - 1)
-    doubles(0, PARTS - 1)
+        cross(hf)
+    for hf in range(PARTS):
+        doubles(0, hf)
     for hf in range(PARTS):
         for i in (2, 3, 4, 5):
             sums[(0, hf), i].wait_recv()

time: 110 us -> 110 us (level)
  no operation moved by 1% of the time
where the time goes in v4:
time: 110 us
  Pallas kernels  109 us (99%)
  local copies, waits for them, and re-layouts  1.77 us (2%)
    pallas_call x1, Pallas kernels, shards(): pl.pallas_call(kernel, out_shape=jax.ShapeDtypeStruct((BLOCK, D), BF), in...  109 us

profile of v4, /device:TPU:1, one launch (start us, length us, event | category | flops | bytes accessed | tf_op | source)
XLA Modules:
  0.0 110.4 jit_solution(16918936937917531908)
XLA Ops:
  0.0 108.6 %frame_attention_grad.1 = bf16[64,3072]{1,0:T(8,128)(2,1)} custom-call(bf16[64,3072]{1,0:T(8,128)(2,1)} %lat_h.1, bf16[64,3072]{1,0:T(8,128)(2,1)} %cot_h.1, f32[1,3072]{1,0:T(1,128)} %bitcast.3, bf16[3,3072,384]{2,1,0:T(8,128)(2,1)} %bitcast.2, bf16[384,3072]{1,0:T(8,128)(2,1)} %wout_h.1), custom_call_target="tpu_custom_call" | custom-call | tf_op jit(solution)/shard_map/frame_attention_grad/pallas_call | solution.py:386
  108.6 1.8 %copy.7 = bf16[64,3072]{1,0:T(8,128)(2,1)} copy(bf16[64,3072]{1,0:T(8,128)(2,1)} %frame_attention_grad.1) | data formatting | bytes 786432

commit v5 on v4

--- a/solution.py
+++ b/solution.py
@@ -147,10 +147,10 @@
     got(0, 3)
     project(1)
     for c in range(4):
+        gather_push(1, 0, 4, c, across)
+    for c in range(4):
         forward(1, 0, c)
     spread(0, 2)
-    for c in range(4):
-        gather_push(1, 0, 4, c, across)
     spread(0, 3)
     for c in range(4):
         forward(0, 1, c)
@@ -164,9 +164,13 @@
     loads[4].wait()
 
     def lanes(h):
+        if isinstance(h, int):
+            return pl.ds(h * HEAD_DIM, HEAD_DIM)
         return pl.ds(pl.multiple_of(h * HEAD_DIM, HEAD_DIM), HEAD_DIM)
 
     def v_lanes(h):
+        if isinstance(h, int):
+            return pl.ds(WIDTH + h * HEAD_DIM, HEAD_DIM)
         return pl.ds(pl.multiple_of(WIDTH + h * HEAD_DIM, HEAD_DIM), HEAD_DIM)
 
     for copy in kv_copies:
@@ -197,8 +201,6 @@
 
     lax.fori_loop(0, 2 * HEADS_HERE, score, 0)
     spread(1, 2)
-    forward(1, 1, 0)
-    forward(1, 1, 1)
     lax.fori_loop(2 * HEADS_HERE, 4 * HEADS_HERE, score, 0)
 
     def score_grads(p, h):
@@ -221,32 +223,34 @@
         lax.fori_loop(0, HEADS_HERE, one, 0)
 
 
-    def backward_first():
+    def grad_attn_first():
         for p in (0, 1):
             ga_f[pl.ds(p * PAIR, PAIR)] = nt(cot[pl.ds(p * PAIR, PAIR)], wo[...]).astype(BF)
 
-        def one(h, carry):
-            rows = pl.ds(0, 2 * PAIR)
-            dp = nt(kv[:, v_lanes(h)], ga_f[:, lanes(h)])
-            for p in (0, 1):
-                pt = probs[p * HEADS_HERE + h]
-                dpp = dp[:, p * PAIR : (p + 1) * PAIR]
-                delta = jnp.sum(pt * dpp, axis=0, keepdims=True)
-                ds_f[:, pl.ds(p * PAIR, PAIR)] = (pt * (dpp - delta) * SCALE).astype(BF)
-                pb_f[:, pl.ds(p * PAIR, PAIR)] = pt.astype(BF)
-            acc_k[:, lanes(h)] = nn(ds_f[...], q[rows, lanes(h)])
-            acc_v[:, lanes(h)] = nn(pb_f[...], ga_f[:, lanes(h)])
-            g[rows, lanes(h)] = nn(kt[h], ds_f[...]).T.astype(BF)
-            return carry
-
-        lax.fori_loop(0, HEADS_HERE, one, 0)
-
-    spread(1, 3)
+    def backward_first(h):
+        rows = pl.ds(0, 2 * PAIR)
+        dp = nt(kv[:, v_lanes(h)], ga_f[:, lanes(h)])
+        for p in (0, 1):
+            pt = probs[p * HEADS_HERE + h]
+            dpp = dp[:, p * PAIR : (p + 1) * PAIR]
+            delta = jnp.sum(pt * dpp, axis=0, keepdims=True)
+            ds_f[:, pl.ds(p * PAIR, PAIR)] = (pt * (dpp - delta) * SCALE).astype(BF)
+            pb_f[:, pl.ds(p * PAIR, PAIR)] = pt.astype(BF)
+        acc_k[:, lanes(h)] = nn(ds_f[...], q[rows, lanes(h)])
+        acc_v[:, lanes(h)] = nn(pb_f[...], ga_f[:, lanes(h)])
+        g[rows, lanes(h)] = nn(kt[h], ds_f[...]).T.astype(BF)
+
+    forward(1, 1, 0)
+    forward(1, 1, 1)
     got(1, 1, (1, 3))
     got(1, 2, (0, 2))
     got(1, 3)
-    backward_first()
+    grad_attn_first()
+    backward_first(0)
+    spread(1, 3)
+    backward_first(1)
     forward(1, 1, 2)
+    backward_first(2)
     forward(1, 1, 3)
     got(1, 5, (1, 3))
     backward(2)
@@ -353,28 +357,23 @@
         cross(hf)
     for hf in range(PARTS):
         doubles(0, hf)
-    for hf in range(PARTS):
+    own_rows = pl.ds(0, BLOCK)
+    scale = inv[:, pl.ds(0, 1)]
+    inner = jnp.zeros((BLOCK, 1), F32)
+    for hf in range(PARTS):
+        cols = pl.ds(hf * COLS, COLS)
         for i in (2, 3, 4, 5):
             sums[(0, hf), i].wait_recv()
-    for hf in range(PARTS):
         crossing[hf].wait_recv()
-
-    for r in range(4):
-        rows = pl.ds(r * 16, 16)
-        scale = inv[rows, pl.ds(0, 1)]
-        inner = jnp.zeros((16, 1), F32)
-        for hf in range(PARTS):
-            cols = pl.ds(hf * COLS, COLS)
-            total = (
-                part[hf, rows].astype(F32) + rl[hf, rows].astype(F32) + rr[hf, rows].astype(F32)
-                + rz[hf, rows].astype(F32)
-            )
-            total = total * gain[:, cols]
-            inner += jnp.sum(total * (lat[rows, cols].astype(F32) * scale), axis=-1, keepdims=True)
-            grad[rows, cols] = total
-        inner = inner * (1.0 / D)
-        normed = lat[rows].astype(F32) * scale
-        out_ref[rows] = (cot[rows].astype(F32) + scale * (grad[rows] - normed * inner)).astype(BF)
+        total = part[hf, own_rows].astype(F32) + rl[hf].astype(F32) + rr[hf].astype(F32) + rz[hf].astype(F32)
+        total = total * gain[:, cols]
+        inner += jnp.sum(total * (lat[:, cols].astype(F32) * scale), axis=-1, keepdims=True)
+        grad[:, cols] = total
+    inner = inner * (1.0 / D)
+    for hf in range(PARTS):
+        cols = pl.ds(hf * COLS, COLS)
+        normed = lat[:, cols].astype(F32) * scale
+        out_ref[:, cols] = (cot[own_rows, cols].astype(F32) + scale * (grad[:, cols] - normed * inner)).astype(BF)
 
     for copy in sent:
         copy.wait_send()

time: 110 us -> 112 us (1.018)
    pallas_call x1, Pallas kernels: 109 us -> 110 us  [shards(): pl.pallas_call(kernel, out_shape=jax.ShapeDtypeStruct((BLOCK, D), BF), in...]
where the time goes in v5:
time: 112 us
  Pallas kernels  110 us (98%)
  local copies, waits for them, and re-layouts  1.77 us (2%)
    pallas_call x1, Pallas kernels, shards(): pl.pallas_call(kernel, out_shape=jax.ShapeDtypeStruct((BLOCK, D), BF), in...  110 us

profile of v5, /device:TPU:1, one launch (start us, length us, event | category | flops | bytes accessed | tf_op | source)
XLA Modules:
  0.0 112.0 jit_solution(9633041014555193389)
XLA Ops:
  0.0 110.2 %frame_attention_grad.1 = bf16[64,3072]{1,0:T(8,128)(2,1)} custom-call(bf16[64,3072]{1,0:T(8,128)(2,1)} %lat_h.1, bf16[64,3072]{1,0:T(8,128)(2,1)} %cot_h.1, f32[1,3072]{1,0:T(1,128)} %bitcast.3, bf16[3,3072,384]{2,1,0:T(8,128)(2,1)} %bitcast.2, bf16[384,3072]{1,0:T(8,128)(2,1)} %wout_h.1), custom_call_target="tpu_custom_call" | custom-call | tf_op jit(solution)/shard_map/frame_attention_grad/pallas_call | solution.py:385
  110.2 1.8 %copy.7 = bf16[64,3072]{1,0:T(8,128)(2,1)} copy(bf16[64,3072]{1,0:T(8,128)(2,1)} %frame_attention_grad.1) | data formatting | bytes 786432

commit v6 on v5

--- a/solution.py
+++ b/solution.py
@@ -136,24 +136,25 @@
     loads[2].wait()
     for c in range(4):
         forward(0, 0, c)
-        to_right(1, 0, (0, 2, 1, 3)[c])
-        to_left(1, 0, (1, 3, 0, 2)[c])
+        (to_left if c % 2 else to_right)(1, 0, c)
     loads[3].wait()
     got(0, 1, (1, 3))
     project(0)
     spread(0, 0)
     spread(0, 1)
+    for c in range(4):
+        (to_right if c % 2 else to_left)(1, 0, c)
     got(0, 2, (0, 2))
     got(0, 3)
     project(1)
+    spread(0, 2)
     for c in range(4):
         gather_push(1, 0, 4, c, across)
+    spread(0, 3)
+    for c in range(4):
+        forward(0, 1, c)
     for c in range(4):
         forward(1, 0, c)
-    spread(0, 2)
-    spread(0, 3)
-    for c in range(4):
-        forward(0, 1, c)
     got(0, 5, (1, 3))
     project(2)
     spread(1, 0)
@@ -173,31 +174,48 @@
             return pl.ds(WIDTH + h * HEAD_DIM, HEAD_DIM)
         return pl.ds(pl.multiple_of(WIDTH + h * HEAD_DIM, HEAD_DIM), HEAD_DIM)
 
+    def turn(rows):
+        def one(h, carry):
+            kt[h, :, rows] = kv[rows, lanes(h)].astype(F32).T.astype(BF)
+            return carry
+
+        lax.fori_loop(0, HEADS_HERE, one, 0)
+
+    own = pl.ds(0, FRAME)
+    prev = pl.ds(FRAME, FRAME)
+
+    def queries_of(i):
+        p = i // HEADS_HERE
+        h = i - p * HEADS_HERE
+        return h, q[pl.ds(pl.multiple_of(p * PAIR, PAIR), PAIR), lanes(h)]
+
+    def score_own(i, carry):
+        h, qh = queries_of(i)
+        probs[i, own] = nt(kv[own, lanes(h)], qh) * SCALE
+        return carry
+
+    def score(i, carry):
+        h, qh = queries_of(i)
+        own_s = probs[i, own]
+        prev_s = jnp.where(tm > 0, nt(kv[prev, lanes(h)], qh) * SCALE, -1e30)
+        top = jnp.maximum(jnp.max(own_s, axis=0, keepdims=True), jnp.max(prev_s, axis=0, keepdims=True))
+        own_e = jnp.exp(own_s - top)
+        prev_e = jnp.exp(prev_s - top)
+        part_of = 1.0 / (jnp.sum(own_e, axis=0, keepdims=True) + jnp.sum(prev_e, axis=0, keepdims=True))
+        probs[i, own] = own_e * part_of
+        probs[i, prev] = prev_e * part_of
+        return carry
+
+    lax.fori_loop(0, 4 * HEADS_HERE, score_own, 0)
+    turn(own)
+    got(1, 1, (1, 3))
+    got(1, 2, (0, 2))
+    got(1, 3)
+    for p in (0, 1):
+        ga_f[pl.ds(p * PAIR, PAIR)] = nt(cot[pl.ds(p * PAIR, PAIR)], wo[...]).astype(BF)
     for copy in kv_copies:
         copy.wait_recv()
-
-    def turn(h, carry):
-        kt[h] = kv[:, lanes(h)].astype(F32).T.astype(BF)
-        return carry
-
-    lax.fori_loop(0, HEADS_HERE, turn, 0)
-
-    def score(i, carry):
-        p = i // HEADS_HERE
-        h = i - p * HEADS_HERE
-        rows = pl.ds(pl.multiple_of(p * PAIR, PAIR), PAIR)
-        qh = q[rows, lanes(h)]
-        own = nt(kv[pl.ds(0, FRAME), lanes(h)], qh) * SCALE
-        prev = nt(kv[pl.ds(FRAME, FRAME), lanes(h)], qh) * SCALE
-        prev = jnp.where(tm > 0, prev, -1e30)
-        top = jnp.maximum(jnp.max(own, axis=0, keepdims=True), jnp.max(prev, axis=0, keepdims=True))
-        own = jnp.exp(own - top)
-        prev = jnp.exp(prev - top)
-        total = jnp.sum(own, axis=0, keepdims=True) + jnp.sum(prev, axis=0, keepdims=True)
-        part_of = 1.0 / total
-        probs[i, pl.ds(0, FRAME)] = own * part_of
-        probs[i, pl.ds(FRAME, FRAME)] = prev * part_of
-        return carry
+    turn(prev)
 
     lax.fori_loop(0, 2 * HEADS_HERE, score, 0)
     spread(1, 2)
@@ -222,10 +240,6 @@
 
         lax.fori_loop(0, HEADS_HERE, one, 0)
 
-
-    def grad_attn_first():
-        for p in (0, 1):
-            ga_f[pl.ds(p * PAIR, PAIR)] = nt(cot[pl.ds(p * PAIR, PAIR)], wo[...]).astype(BF)
 
     def backward_first(h):
         rows = pl.ds(0, 2 * PAIR)
@@ -242,10 +256,6 @@
 
     forward(1, 1, 0)
     forward(1, 1, 1)
-    got(1, 1, (1, 3))
-    got(1, 2, (0, 2))
-    got(1, 3)
-    grad_attn_first()
     backward_first(0)
     spread(1, 3)
     backward_first(1)
@@ -258,8 +268,6 @@
     got(1, 7)
 
     last = pl.ds(3 * PAIR, PAIR)
-    own = pl.ds(0, FRAME)
-    prev = pl.ds(FRAME, FRAME)
     ga_s[...] = nt(cot[last], wo[...]).astype(BF)
 
     def last_prev(h, carry):

time: 112 us -> 109 us (0.973)
  Pallas kernels: 110 us -> 107 us
    pallas_call x1, Pallas kernels: 110 us -> 107 us  [shards(): pl.pallas_call(kernel, out_shape=jax.ShapeDtypeStruct((BLOCK, D), BF), in...]
where the time goes in v6:
time: 109 us
  Pallas kernels  107 us (98%)
  local copies, waits for them, and re-layouts  1.77 us (2%)
    pallas_call x1, Pallas kernels, shards(): pl.pallas_call(kernel, out_shape=jax.ShapeDtypeStruct((BLOCK, D), BF), in...  107 us

profile of v6, /device:TPU:1, one launch (start us, length us, event | category | flops | bytes accessed | tf_op | source)
XLA Modules:
  0.0 108.9 jit_solution(7155753617933766239)
XLA Ops:
  0.0 107.1 %frame_attention_grad.1 = bf16[64,3072]{1,0:T(8,128)(2,1)} custom-call(bf16[64,3072]{1,0:T(8,128)(2,1)} %lat_h.1, bf16[64,3072]{1,0:T(8,128)(2,1)} %cot_h.1, f32[1,3072]{1,0:T(1,128)} %bitcast.3, bf16[3,3072,384]{2,1,0:T(8,128)(2,1)} %bitcast.2, bf16[384,3072]{1,0:T(8,128)(2,1)} %wout_h.1), custom_call_target="tpu_custom_call" | custom-call | tf_op jit(solution)/shard_map/frame_attention_grad/pallas_call | solution.py:393
  107.1 1.8 %copy.7 = bf16[64,3072]{1,0:T(8,128)(2,1)} copy(bf16[64,3072]{1,0:T(8,128)(2,1)} %frame_attention_grad.1) | data formatting | bytes 786432

commit v7 on v6

--- a/solution.py
+++ b/solution.py
@@ -39,7 +39,7 @@
     lat_h, cot_h, gain_h, wqkv_h, wout_h, out_ref,
     lat, gain, wq, wo, hid, cot, inv, q, kv, kt, probs, acc_k, acc_v, back_s, back_r, g,
     part, ra, rb, rl, rr, zs, rz, ga_s, ds_s, ga_f, ds_f, pb_f, grad,
-    ld_sem, gs_sem, gr_sem, kvs_sem, kvr_sem, bs_sem, br_sem, rs_sem, rr_sem, zs_sem, zr_sem,
+    ld_sem, gs_sem, gr_sem, kvs_sem, kvr_sem, bs_sem, br_sem, rs_sem, rr_sem, zs_sem, zr_sem, z_ready, tm_ready,
 ):
     tm = lax.axis_index("tm")
     head = lax.axis_index("head")
@@ -52,8 +52,12 @@
     before = (lax.rem(tm + N_TM - 1, N_TM), head)
 
     barrier = pltpu.get_barrier_semaphore()
-    for peer in (right, left, across, after, before):
+    for peer in (right, left, before):
         pl.semaphore_signal(barrier, inc=1, device_id=peer, device_id_type=MESH)
+
+    @pl.when(head < X)
+    def _():
+        pl.semaphore_signal(barrier, inc=1, device_id=across, device_id_type=MESH)
 
     loads = [
         pltpu.make_async_copy(lat_h, lat, ld_sem.at[0]),
@@ -72,7 +76,16 @@
         scale = lax.rsqrt(jnp.mean(lf * lf, axis=-1, keepdims=True) + EPSILON)
         inv[rows] = jnp.broadcast_to(scale, (16, 128))
         hid[rows] = (lf * scale * gain[...]).astype(BF)
-    pl.semaphore_wait(barrier, 5)
+    @pl.when(head < X)
+    def _():
+        pl.semaphore_wait(barrier, 3)
+
+    @pl.when(head >= X)
+    def _():
+        pl.semaphore_wait(barrier, 4)
+        pl.semaphore_signal(z_ready, inc=1, device_id=across, device_id_type=MESH)
+
+    pl.semaphore_signal(tm_ready, inc=1, device_id=after, device_id_type=MESH)
 
     sent = []
 
@@ -130,9 +143,15 @@
         )
 
     for c in range(4):
-        gather_push(0, 0, 4, c, across)
         to_right(0, 0, (0, 2, 1, 3)[c])
         to_left(0, 0, (1, 3, 0, 2)[c])
+
+    @pl.when(head < X)
+    def _():
+        pl.semaphore_wait(z_ready, 1)
+
+    for c in range(4):
+        gather_push(0, 0, 4, c, across)
     loads[2].wait()
     for c in range(4):
         forward(0, 0, c)
@@ -279,6 +298,7 @@
 
     lax.fori_loop(0, HEADS_HERE, last_prev, 0)
     pieces = ((448, 64), (256, 192), (0, 256))
+    pl.semaphore_wait(tm_ready, 1)
     backs = []
     for i, (start, size) in enumerate(pieces):
         rows = pl.ds(start, size)
@@ -357,12 +377,14 @@
         partials(1, hf)
         singles(1, hf)
         doubles(1, hf)
+    cross(0)
     join(2)
     for hf in range(PARTS):
         partials(2, hf)
         opposite(0, hf)
         singles(0, hf)
-        cross(hf)
+        if hf + 1 < PARTS:
+            cross(hf + 1)
     for hf in range(PARTS):
         doubles(0, hf)
     own_rows = pl.ds(0, BLOCK)
@@ -436,6 +458,8 @@
             dma((12 * PARTS,)),
             dma((PARTS,)),
             dma((PARTS,)),
+            pltpu.SemaphoreType.REGULAR,
+            pltpu.SemaphoreType.REGULAR,
         ],
         compiler_params=pltpu.CompilerParams(
             collective_id=0, has_side_effects=True, vmem_limit_bytes=56 * 1024 * 1024

time: 109 us -> 108 us (level); the launches traced: 109 us -> 107 us
  Pallas kernels: 107 us -> 105 us
    pallas_call x1, Pallas kernels: 107 us -> 105 us  [shards(): pl.pallas_call(kernel, out_shape=jax.ShapeDtypeStruct((BLOCK, D), BF), in...]
where the time goes in v7:
time: 108 us; the launch traced here: 107 us
  Pallas kernels  105 us (97%)
  local copies, waits for them, and re-layouts  1.77 us (2%)
    pallas_call x1, Pallas kernels, shards(): pl.pallas_call(kernel, out_shape=jax.ShapeDtypeStruct((BLOCK, D), BF), in...  105 us

profile of v7, /device:TPU:1, one launch (start us, length us, event | category | flops | bytes accessed | tf_op | source)
XLA Modules:
  0.0 106.5 jit_solution(13339291666303195018)
XLA Ops:
  0.0 104.8 %frame_attention_grad.1 = bf16[64,3072]{1,0:T(8,128)(2,1)} custom-call(bf16[64,3072]{1,0:T(8,128)(2,1)} %lat_h.1, bf16[64,3072]{1,0:T(8,128)(2,1)} %cot_h.1, f32[1,3072]{1,0:T(1,128)} %bitcast.3, bf16[3,3072,384]{2,1,0:T(8,128)(2,1)} %bitcast.2, bf16[384,3072]{1,0:T(8,128)(2,1)} %wout_h.1), custom_call_target="tpu_custom_call" | custom-call | tf_op jit(solution)/shard_map/frame_attention_grad/pallas_call | solution.py:415
  104.8 1.8 %copy.7 = bf16[64,3072]{1,0:T(8,128)(2,1)} copy(bf16[64,3072]{1,0:T(8,128)(2,1)} %frame_attention_grad.1) | data formatting | bytes 786432

commit v8 on v7

--- a/solution.py
+++ b/solution.py
@@ -36,10 +36,10 @@
 
 
 def kernel(
-    lat_h, cot_h, gain_h, wqkv_h, wout_h, out_ref,
+    lat_h, cot_h, gain_h, wqkv_h, wout_h, out_h,
     lat, gain, wq, wo, hid, cot, inv, q, kv, kt, probs, acc_k, acc_v, back_s, back_r, g,
     part, ra, rb, rl, rr, zs, rz, ga_s, ds_s, ga_f, ds_f, pb_f, grad,
-    ld_sem, gs_sem, gr_sem, kvs_sem, kvr_sem, bs_sem, br_sem, rs_sem, rr_sem, zs_sem, zr_sem, z_ready, tm_ready,
+    ld_sem, gs_sem, gr_sem, kvs_sem, kvr_sem, bs_sem, br_sem, rs_sem, rr_sem, zs_sem, zr_sem, z_ready, tm_ready, out_v, out_sem,
 ):
     tm = lax.axis_index("tm")
     head = lax.axis_index("head")
@@ -97,6 +97,11 @@
         sent.append(copy)
         return copy
 
+    def settle(n):
+        for copy in sent[:n]:
+            copy.wait_send()
+        del sent[:n]
+
     def chunk(slot, c):
         return pl.ds(slot * BLOCK + c * HALF, HALF)
 
@@ -292,17 +297,35 @@
     def last_prev(h, carry):
         pt, ds = score_grads(3, h)
         ds_s[h] = ds
-        back_s[:, lanes(h)] = (acc_k[prev, lanes(h)] + nn(ds[FRAME:], q[last, lanes(h)])).astype(BF)
-        back_s[:, v_lanes(h)] = (acc_v[prev, lanes(h)] + nn(pt[FRAME:].astype(BF), ga_s[:, lanes(h)])).astype(BF)
+        back_piece(h, *pieces[0])
         return carry
 
+    def back_piece(h, start, size):
+        theirs = pl.ds(FRAME + start, size)
+        ours = pl.ds(start, size)
+        weights = probs[3 * HEADS_HERE + h, theirs].astype(BF)
+        back_s[ours, lanes(h)] = (acc_k[theirs, lanes(h)] + nn(ds_s[h, theirs], q[last, lanes(h)])).astype(BF)
+        back_s[ours, v_lanes(h)] = (acc_v[theirs, lanes(h)] + nn(weights, ga_s[:, lanes(h)])).astype(BF)
+
+    pieces = ((448, 64), (256, 192), (0, 256))
+    n_gather = len(sent)
+    backs = []
+
+    def send_back(i):
+        rows = pl.ds(*pieces[i])
+        backs.append(push(back_s.at[rows], back_r.at[rows], bs_sem.at[i], br_sem.at[i], before))
+
     lax.fori_loop(0, HEADS_HERE, last_prev, 0)
-    pieces = ((448, 64), (256, 192), (0, 256))
     pl.semaphore_wait(tm_ready, 1)
-    backs = []
-    for i, (start, size) in enumerate(pieces):
-        rows = pl.ds(start, size)
-        backs.append(push(back_s.at[rows], back_r.at[rows], bs_sem.at[i], br_sem.at[i], before))
+    send_back(0)
+    for i in (1, 2):
+
+        def rest(h, carry):
+            back_piece(h, *pieces[i])
+            return carry
+
+        lax.fori_loop(0, HEADS_HERE, rest, 0)
+        send_back(i)
 
     def last_own(h, carry):
         g[last, lanes(h)] = nn(kt[h], ds_s[h]).T.astype(BF)
@@ -368,6 +391,7 @@
         zs[hf] = (mine + rl[PARTS + hf].astype(F32) + rr[PARTS + hf].astype(F32)).astype(BF)
         crossing[hf] = push(zs.at[hf], rz.at[hf], zs_sem.at[hf], zr_sem.at[hf], across)
 
+    settle(n_gather)
     join(0)
     for hf in range(PARTS):
         partials(0, hf)
@@ -377,6 +401,7 @@
         partials(1, hf)
         singles(1, hf)
         doubles(1, hf)
+    n_first = len(sent)
     cross(0)
     join(2)
     for hf in range(PARTS):
@@ -387,6 +412,7 @@
             cross(hf + 1)
     for hf in range(PARTS):
         doubles(0, hf)
+    settle(n_first)
     own_rows = pl.ds(0, BLOCK)
     scale = inv[:, pl.ds(0, 1)]
     inner = jnp.zeros((BLOCK, 1), F32)
@@ -400,13 +426,17 @@
         inner += jnp.sum(total * (lat[:, cols].astype(F32) * scale), axis=-1, keepdims=True)
         grad[:, cols] = total
     inner = inner * (1.0 / D)
+    outs = []
     for hf in range(PARTS):
         cols = pl.ds(hf * COLS, COLS)
         normed = lat[:, cols].astype(F32) * scale
-        out_ref[:, cols] = (cot[own_rows, cols].astype(F32) + scale * (grad[:, cols] - normed * inner)).astype(BF)
-
-    for copy in sent:
-        copy.wait_send()
+        out_v[hf] = (cot[own_rows, cols].astype(F32) + scale * (grad[:, cols] - normed * inner)).astype(BF)
+        outs.append(pltpu.make_async_copy(out_v.at[hf], out_h.at[:, cols], out_sem.at[hf]))
+        outs[-1].start()
+
+    settle(len(sent))
+    for copy in outs:
+        copy.wait()
 
 
 def shards(latents, cotangent, norm_gain, w_qkv, w_out):
@@ -416,7 +446,7 @@
         kernel,
         out_shape=jax.ShapeDtypeStruct((BLOCK, D), BF),
         in_specs=[hbm] * 5,
-        out_specs=pl.BlockSpec(memory_space=pltpu.VMEM),
+        out_specs=hbm,
         scratch_shapes=[
             pltpu.VMEM((BLOCK, D), BF),
             pltpu.VMEM((1, D), F32),
@@ -460,6 +490,8 @@
             dma((PARTS,)),
             pltpu.SemaphoreType.REGULAR,
             pltpu.SemaphoreType.REGULAR,
+            pltpu.VMEM((PARTS, BLOCK, COLS), BF),
+            dma((PARTS,)),
         ],
         compiler_params=pltpu.CompilerParams(
             collective_id=0, has_side_effects=True, vmem_limit_bytes=56 * 1024 * 1024

time: 108 us -> 108 us (level)
  no operation moved by 1% of the time
where the time goes in v8:
time: 108 us; the launch traced here: 106 us
  Pallas kernels  104 us (96%)
  local copies, waits for them, and re-layouts  1.77 us (2%)
    pallas_call x1, Pallas kernels, shards(): pl.pallas_call(kernel, out_shape=jax.ShapeDtypeStruct((BLOCK, D), BF), in...  104 us

profile of v8, /device:TPU:1, one launch (start us, length us, event | category | flops | bytes accessed | tf_op | source)
XLA Modules:
  0.0 105.8 jit_solution(10226702146742103049)
XLA Ops:
  0.0 104.0 %frame_attention_grad.1 = bf16[64,3072]{1,0:T(8,128)(2,1)} custom-call(bf16[64,3072]{1,0:T(8,128)(2,1)} %lat_h.1, bf16[64,3072]{1,0:T(8,128)(2,1)} %cot_h.1, f32[1,3072]{1,0:T(1,128)} %bitcast.3, bf16[3,3072,384]{2,1,0:T(8,128)(2,1)} %bitcast.2, bf16[384,3072]{1,0:T(8,128)(2,1)} %wout_h.1), custom_call_target="tpu_custom_call" | custom-call | tf_op jit(solution)/shard_map/frame_attention_grad/pallas_call | solution.py:445
  104.0 1.8 %copy.7 = bf16[64,3072]{1,0:T(8,128)(2,1)} copy(bf16[64,3072]{1,0:T(8,128)(2,1)} %frame_attention_grad.1) | data formatting | bytes 786432

commit v9 on v8

--- a/solution.py
+++ b/solution.py
@@ -171,9 +171,9 @@
     got(0, 2, (0, 2))
     got(0, 3)
     project(1)
+    for c in range(4):
+        gather_push(1, 0, 4, c, across)
     spread(0, 2)
-    for c in range(4):
-        gather_push(1, 0, 4, c, across)
     spread(0, 3)
     for c in range(4):
         forward(0, 1, c)

time: 108 us -> 108 us (level)
  no operation moved by 1% of the time
where the time goes in v9:
time: 108 us; the launch traced here: 106 us
  Pallas kernels  104 us (96%)
  local copies, waits for them, and re-layouts  1.77 us (2%)
    pallas_call x1, Pallas kernels, shards(): pl.pallas_call(kernel, out_shape=jax.ShapeDtypeStruct((BLOCK, D), BF), in...  104 us

profile of v9, /device:TPU:1, one launch (start us, length us, event | category | flops | bytes accessed | tf_op | source)
XLA Modules:
  0.0 105.9 jit_solution(14488631040614779012)
XLA Ops:
  0.0 104.1 %frame_attention_grad.1 = bf16[64,3072]{1,0:T(8,128)(2,1)} custom-call(bf16[64,3072]{1,0:T(8,128)(2,1)} %lat_h.1, bf16[64,3072]{1,0:T(8,128)(2,1)} %cot_h.1, f32[1,3072]{1,0:T(1,128)} %bitcast.3, bf16[3,3072,384]{2,1,0:T(8,128)(2,1)} %bitcast.2, bf16[384,3072]{1,0:T(8,128)(2,1)} %wout_h.1), custom_call_target="tpu_custom_call" | custom-call | tf_op jit(solution)/shard_map/frame_attention_grad/pallas_call | solution.py:445
  104.1 1.8 %copy.7 = bf16[64,3072]{1,0:T(8,128)(2,1)} copy(bf16[64,3072]{1,0:T(8,128)(2,1)} %frame_attention_grad.1) | data formatting | bytes 786432
